TPU v7x, 512 devices: a whole 4x8x8 slice. The times are simulated.
512 devices in a mesh: dp: 64 (over y, z), feat: 8 (over x, core).
Axes of the slice: x: 4, y: 8, z: 8, core: 2. Of those that a mesh axis runs over, the one named last changes fastest.
Arguments:
- table: float32 [32768, 768], P('dp', 'feat'), may hold values from -6 to 6
- node_ids: int32 [65536], P('dp'), may hold values from 0 to 511
- tiles: int32 [512, 128, 128], P('dp'), may hold values 0 or 1
- tile_rows: int32 [512], P('dp'), may hold values from 0 to 1
- tile_cols: int32 [512], P('dp'), may hold values from 0 to 7, as said below
- tile_count: int32 [64], P('dp'), may hold values from 6 to 8, as said below
- seed_count: int32 [64], P('dp'), may hold values from 128 to 256, as said below
- w_self: float32 [768, 1024], P('feat'), may hold values from -0.21875 to 0.21875
- w_neigh: float32 [768, 1024], P('feat'), may hold values from -0.21875 to 0.21875
- bias: float32 [1024], P('feat'), may hold values from -3 to 3
- cotangent: bfloat16 [16384, 1024], P('dp', 'feat'), may hold values from -0.046875 to 0.046875
Outputs:
- hidden: bfloat16 [16384, 1024], P('dp', 'feat')
- grad_self: float32 [768, 1024], P('feat')
- grad_neigh: float32 [768, 1024], P('feat')
- grad_bias: float32 [1024], P('feat')
Inputs may be any that keep to these rules, and one draw needn't show every extreme that they name: `node_ids`: entry k of a dp index's 1024 entries is a row within the block of 512 table rows held by dp index k // 16; repeats occur. `tile_rows`: tiles may share coordinates; their edges then add. `tile_cols`: each of a dp index's 6 sampled blocks past its targets is the column block of at least one of its live tiles. A dp index uses its first tile_count tiles; some index uses all 8. A dp index's first seed_count targets are live; some index has all 256.
All inputs are finite; a program needn't handle non-finite values. No bound on the sum of `tiles` on one device may be relied on, other than what follows from the above.
Results may differ from a plain program's by a relative error of at most 0.007.
Values may be sent and summed in bfloat16 or wider, within the bound.
A program may use at most 64 MiB of HBM per device.

v0:
```python
import jax
import jax.numpy as jnp
from jax import lax
from jax.sharding import PartitionSpec as P


def on_device(
    table,
    node_ids,
    tiles,
    tile_rows,
    tile_cols,
    tile_count,
    seed_count,
    w_self,
    w_neigh,
    bias,
    cotangent,
):
    highest = lax.Precision.HIGHEST
    devices = lax.axis_size("dp")
    samples = node_ids.shape[0]
    slot_count = samples // devices
    block_size = tiles.shape[1]
    targets = cotangent.shape[0]
    feature_cols = table.shape[1]
    requests_grid = node_ids.reshape(devices, slot_count)
    found_rows = table[lax.all_to_all(requests_grid, "dp", split_axis=0, concat_axis=0, tiled=True)]
    sampled = lax.all_to_all(found_rows, "dp", split_axis=0, concat_axis=0, tiled=True).reshape(
        samples, feature_cols
    )

    def add_tile(step, state):
        summed, degree = state
        tile_block = tiles[step].astype(jnp.float32)
        sources = lax.dynamic_slice_in_dim(sampled, tile_cols[step] * block_size, block_size, 0)
        start = tile_rows[step] * block_size
        product = jnp.dot(tile_block, sources, precision=highest)
        summed = lax.dynamic_update_slice_in_dim(
            summed, lax.dynamic_slice_in_dim(summed, start, block_size, 0) + product, start, 0
        )
        row_sums = jnp.sum(tile_block, axis=1)
        degree = lax.dynamic_update_slice_in_dim(
            degree, lax.dynamic_slice_in_dim(degree, start, block_size, 0) + row_sums, start, 0
        )
        return (summed, degree)

    start_state = (
        jnp.zeros((targets, feature_cols), jnp.float32),
        jnp.zeros((targets,), jnp.float32),
    )
    summed, degree = lax.fori_loop(0, tile_count[0], add_tile, start_state)
    neighbour_mean = summed / jnp.maximum(degree, 1.0)[:, None]
    self_rows = sampled[:targets]
    alive = (lax.iota(jnp.int32, targets) < seed_count[0]).astype(jnp.float32)[:, None]
    full_self, full_neigh = (
        lax.all_gather(self_rows, "feat", axis=1, tiled=True),
        lax.all_gather(neighbour_mean, "feat", axis=1, tiled=True),
    )
    slab_self, slab_neigh = (
        lax.all_to_all(w_self, "feat", split_axis=1, concat_axis=0, tiled=True),
        lax.all_to_all(w_neigh, "feat", split_axis=1, concat_axis=0, tiled=True),
    )
    preact = (
        jnp.dot(full_self, slab_self, precision=highest)
        + jnp.dot(full_neigh, slab_neigh, precision=highest)
        + bias
    )
    sigma = jax.nn.sigmoid(preact)
    hidden = (preact * sigma * alive).astype(jnp.bfloat16)
    slope = (cotangent.astype(jnp.float32) * alive * sigma * (1.0 + preact * (1.0 - sigma))).astype(
        jnp.bfloat16
    )
    hidden, slope = (hidden, slope)
    slope_wide = slope.astype(jnp.float32)
    part_self = jnp.dot(full_self.T, slope_wide, precision=highest)
    part_neigh = jnp.dot(full_neigh.T, slope_wide, precision=highest)
    grad_self, grad_neigh = (
        lax.all_to_all(part_self, "feat", split_axis=0, concat_axis=1, tiled=True),
        lax.all_to_all(part_neigh, "feat", split_axis=0, concat_axis=1, tiled=True),
    )
    grad_bias = jnp.sum(slope_wide, axis=0)
    grad_self, grad_neigh, grad_bias = lax.psum((grad_self, grad_neigh, grad_bias), "dp")
    return (hidden, grad_self, grad_neigh, grad_bias)


def solution(mesh):
    placed = (
        P("dp", "feat"),
        P("dp"),
        P("dp", None, None),
        P("dp"),
        P("dp"),
        P("dp"),
        P("dp"),
        P("feat", None),
        P("feat", None),
        P("feat"),
        P("dp", "feat"),
    )
    return jax.shard_map(
        on_device,
        mesh=mesh,
        in_specs=placed,
        out_specs=(P("dp", "feat"), P("feat", None), P("feat", None), P("feat")),
        check_vma=False,
    )
```

profile of v0, /device:TPU:6, one launch (start us, length us, event | category | flops | bytes accessed | tf_op | source)
XLA Modules:
  0.0 338.1 jit_solution(17209903225781210375)
XLA Ops:
  7.2 1.4 all_to_all.67
  8.6 16.6 %all-to-all-start = ((s32[64,1,16]{2,1,0:T(1,128)}), s32[64,1,16]{2,1,0:T(1,128)S(1)}, u32[]{:S(2)}, u32[]{:S(2)}) async-start(s32[64,1,16]{2,1,0:T(1,128)} %bitcast.3), calls=%async_computation | async-start | bytes 65536 | tf_op jit(solution)/shard_map/all_to_all | solution.py:28
  25.2 1.1 copy.34
  26.3 10.8 %all-to-all-done = s32[64,1,16]{2,1,0:T(1,128)S(1)} async-done(((s32[64,1,16]{2,1,0:T(1,128)}), s32[64,1,16]{2,1,0:T(1,128)S(1)}, u32[]{:S(2)}, u32[]{:S(2)}) %all-to-all-start) | async-done | bytes 4128 | tf_op jit(solution)/shard_map/all_to_all | solution.py:28
  37.2 4.0 %gather_fusion = f32[1024,96]{1,0:T(8,128)} fusion(f32[512,96]{1,0:T(8,128)S(1)} %copy.34, s32[1024]{0:T(1024)S(1)} %broadcast_clamp_fusion), kind=kCustom, calls=%fused_computation | custom fusion | bytes 790528 | tf_op jit(solution)/shard_map/gather | solution.py:28
  41.2 4.6 %all-to-all-start.1 = ((f32[64,16,96]{2,1,0:T(8,128)}), f32[64,16,96]{2,1,0:T(8,128)S(1)}, u32[]{:S(2)}, u32[]{:S(2)}) async-start(f32[64,16,96]{2,1,0:T(8,128)} %bitcast.5), calls=%async_computation.1 | async-start | bytes 1048576 | tf_op jit(solution)/shard_map/all_to_all | solution.py:29
  48.4 15.7 %all-to-all-done.1 = f32[64,16,96]{2,1,0:T(8,128)S(1)} async-done(((f32[64,16,96]{2,1,0:T(8,128)}), f32[64,16,96]{2,1,0:T(8,128)S(1)}, u32[]{:S(2)}, u32[]{:S(2)}) %all-to-all-start.1) | async-done | bytes 393248 | tf_op jit(solution)/shard_map/all_to_all | solution.py:29
  64.2 4.8 %all-to-all-start.2 = ((f32[96,8,128]{2,0,1:T(8,128)}), f32[96,8,128]{2,0,1:T(8,128)S(1)}, u32[]{:S(2)}, u32[]{:S(2)}) async-start(f32[96,8,128]{2,0,1:T(8,128)} %copy_bitcast_fusion.3), calls=%async_computation.2 | async-start | bytes 786432 | tf_op jit(solution)/shard_map/all_to_all | solution.py:61
  69.6 33.1 %while.12 = (s32[]{:T(128)}, f32[256,96]{0,1:T(8,128)S(1)}, f32[256]{0:T(256)S(1)}, s32[]{:T(128)}, s32[8]{0:T(128)S(1)}, /*index=5*/s32[8,128,128]{2,1,0:T(8,12...) while((s32[]{:T(128)}, f32[256,96]{0,1:T(8,128)S(1)}, ...), condition=%wide.region_2.0_spmd, body=%wide.region_0.0_spmd.sunk | while | flops 18935820 | bytes 297271 | solution.py:52
  72.8 0.9 convert_reduce_fusion.3
  73.9 1.1 fusion.27
  78.2 0.9 convert_reduce_fusion.3
  79.3 1.1 fusion.27
  83.6 0.9 convert_reduce_fusion.3
  84.7 1.1 fusion.27
  90.1 1.1 fusion.27
  95.5 1.1 fusion.27
  100.9 1.1 fusion.27
  102.8 13.5 %all_gather.6 = f32[256,768]{0,1:T(8,128)S(1)} all-gather(f32[256,96]{0,1:T(8,128)S(1)} %copy.35), channel_id=1, replica_groups=mesh['dp'=64,'feat'=8] {'feat'}, dimensions={1}, use_global_device_ids=true | all-gather | bytes 884736 | tf_op jit(solution)/shard_map/all_gather | solution.py:57
  116.3 4.5 %all-to-all-start.3 = ((f32[96,8,128]{2,0,1:T(8,128)}), f32[96,8,128]{2,0,1:T(8,128)S(1)}, u32[]{:S(2)}, u32[]{:S(2)}) async-start(f32[96,8,128]{2,0,1:T(8,128)} %copy_bitcast_fusion.2), calls=%async_computation.3 | async-start | bytes 786432 | tf_op jit(solution)/shard_map/all_to_all | solution.py:62
  120.8 1.4 fusion.7
  122.2 14.1 %all_gather.7 = f32[256,768]{0,1:T(8,128)S(1)} all-gather(f32[256,96]{0,1:T(8,128)S(1)} %broadcast_divide_fusion), channel_id=1, replica_groups=mesh['dp'=64,'feat'=8] {'feat'}, dimensions={1}, use_global_device_ids=true | all-gather | bytes 884736 | tf_op jit(solution)/shard_map/all_gather | solution.py:58
  137.0 2.1 convert_reduce_fusion.1
  139.0 1.2 fusion.9
  140.3 5.0 %all-to-all-start.5 = ((f32[8,96,128]{2,1,0:T(8,128)}), f32[8,96,128]{2,1,0:T(8,128)S(1)}, u32[]{:S(2)}, u32[]{:S(2)}) async-start(f32[8,96,128]{2,1,0:T(8,128)} %bitcast.16), calls=%async_computation.5 | async-start | bytes 786432 | tf_op jit(solution)/shard_map/all_to_all | solution.py:80
  145.3 1.2 fusion.8
  146.5 5.6 %all-to-all-done.5 = f32[8,96,128]{2,1,0:T(8,128)S(1)} async-done(((f32[8,96,128]{2,1,0:T(8,128)}), f32[8,96,128]{2,1,0:T(8,128)S(1)}, u32[]{:S(2)}, u32[]{:S(2)}) %all-to-all-start.5) | async-done | bytes 393248 | tf_op jit(solution)/shard_map/all_to_all | solution.py:80
  152.2 5.5 %all-to-all-start.4 = ((f32[8,96,128]{2,1,0:T(8,128)}), f32[8,96,128]{2,1,0:T(8,128)S(1)}, u32[]{:S(2)}, u32[]{:S(2)}) async-start(f32[8,96,128]{2,1,0:T(8,128)} %bitcast.14), calls=%async_computation.4 | async-start | bytes 786432 | tf_op jit(solution)/shard_map/all_to_all | solution.py:79
  158.4 6.1 %all-to-all-done.4 = f32[8,96,128]{2,1,0:T(8,128)S(1)} async-done(((f32[8,96,128]{2,1,0:T(8,128)}), f32[8,96,128]{2,1,0:T(8,128)S(1)}, u32[]{:S(2)}, u32[]{:S(2)}) %all-to-all-start.4) | async-done | bytes 393248 | tf_op jit(solution)/shard_map/all_to_all | solution.py:79
  165.3 145.8 %psum.23 = f32[128]{0:T(128)} all-reduce(f32[128]{0:T(128)S(1)} %get-tuple-element.68), channel_id=1, replica_groups=mesh['dp'=64,'feat'=8] {'dp'}, use_global_device_ids=true, to_apply=%region_6.0 | all-reduce | flops 128 | bytes 1024 | tf_op jit(solution)/shard_map/psum | solution.py:83
  311.1 17.6 %all-reduce.3.cloned.1.call-done = (f32[96,1024]{1,0:T(8,128)}, f32[96,1024]{1,0:T(8,128)}) async-done(((f32[96,1024]{1,0:T(8,128)}, f32[96,1024]{1,0:T(8,128)}), (f32[96,1024]{1,0:T(8,128)}, f32[96,1024]{1,0:T(8,128)})) %all-reduce.3.cloned.1.call-update) | async-done | bytes 786448 | tf_op jit(solution)/shard_map/psum | solution.py:83
  328.7 1.8 copy.62
  (54 shorter events, 16.7 us)
Async XLA Ops:
  7.2 39.3 %copy-start = (f32[96,1024]{1,0:T(8,128)S(1)}, f32[96,1024]{1,0:T(8,128)}, u32[]{:S(2)}) copy-start(f32[96,1024]{1,0:T(8,128)} %param.20) | copy-start | bytes 1179652
  8.6 28.5 %all-to-all-start = ((s32[64,1,16]{2,1,0:T(1,128)}), s32[64,1,16]{2,1,0:T(1,128)S(1)}, u32[]{:S(2)}, u32[]{:S(2)}) async-start(s32[64,1,16]{2,1,0:T(1,128)} %bitcast.3), calls=%async_computation | async-start | bytes 65536 | tf_op jit(solution)/shard_map/all_to_all | solution.py:28
  41.2 23.0 %all-to-all-start.1 = ((f32[64,16,96]{2,1,0:T(8,128)}), f32[64,16,96]{2,1,0:T(8,128)S(1)}, u32[]{:S(2)}, u32[]{:S(2)}) async-start(f32[64,16,96]{2,1,0:T(8,128)} %bitcast.5), calls=%async_computation.1 | async-start | bytes 1048576 | tf_op jit(solution)/shard_map/all_to_all | solution.py:29
  46.5 1.1 copy-start.1
  64.2 52.2 %all-to-all-start.2 = ((f32[96,8,128]{2,0,1:T(8,128)}), f32[96,8,128]{2,0,1:T(8,128)S(1)}, u32[]{:S(2)}, u32[]{:S(2)}) async-start(f32[96,8,128]{2,0,1:T(8,128)} %copy_bitcast_fusion.3), calls=%async_computation.2 | async-start | bytes 786432 | tf_op jit(solution)/shard_map/all_to_all | solution.py:61
  68.9 0.7 copy-start.5
  68.9 0.7 copy-start.6
  116.3 20.0 %all-to-all-start.3 = ((f32[96,8,128]{2,0,1:T(8,128)}), f32[96,8,128]{2,0,1:T(8,128)S(1)}, u32[]{:S(2)}, u32[]{:S(2)}) async-start(f32[96,8,128]{2,0,1:T(8,128)} %copy_bitcast_fusion.2), calls=%async_computation.3 | async-start | bytes 786432 | tf_op jit(solution)/shard_map/all_to_all | solution.py:62
  122.2 14.1 %copy-start.3 = (bf16[256,128]{1,0:T(8,128)(2,1)S(1)}, bf16[256,128]{1,0:T(8,128)(2,1)}, u32[]{:S(2)}) copy-start(bf16[256,128]{1,0:T(8,128)(2,1)} %param.23) | copy-start | bytes 196612
  136.3 0.7 copy-start.4
  140.3 11.9 %all-to-all-start.5 = ((f32[8,96,128]{2,1,0:T(8,128)}), f32[8,96,128]{2,1,0:T(8,128)S(1)}, u32[]{:S(2)}, u32[]{:S(2)}) async-start(f32[8,96,128]{2,1,0:T(8,128)} %bitcast.16), calls=%async_computation.5 | async-start | bytes 786432 | tf_op jit(solution)/shard_map/all_to_all | solution.py:80
  152.2 12.3 %all-to-all-start.4 = ((f32[8,96,128]{2,1,0:T(8,128)}), f32[8,96,128]{2,1,0:T(8,128)S(1)}, u32[]{:S(2)}, u32[]{:S(2)}) async-start(f32[8,96,128]{2,1,0:T(8,128)} %bitcast.14), calls=%async_computation.4 | async-start | bytes 786432 | tf_op jit(solution)/shard_map/all_to_all | solution.py:79
  157.6 171.0 %all-reduce.3.cloned.1.call-start = ((), (), s32[]{:S(2)}) async-start(), calls=%async_computation.6 | async-start | bytes 1572864 | tf_op jit(solution)/shard_map/psum | solution.py:83
  328.7 1.8 copy-start.2
Sparse Core Ops, SparseCore 0:
  165.4 163.2 all-reduce.2
where the time goes:
time: 340 us; the launch traced here: 338 us
  blocking collectives  173 us (51%)
  waiting for transfers between devices  55.9 us (16%)
  starting transfers between devices  41 us (12%)
  local copies, waits for them, and re-layouts  21.1 us (6%)
  between operations  14.8 us (4%)
  loops' own time  12.6 us (4%)
  matrix products  12.6 us (4%)
  other arithmetic  6.74 us (2%)
    psum x1, blocking collectives, on_device(): lax.psum((grad_self, grad_neigh, grad_bias), 'dp')  146 us
    psum x1, waiting for transfers between devices, on_device(): lax.psum((grad_self, grad_neigh, grad_bias), 'dp')  17.6 us
    all_to_all x1, starting transfers between devices, on_device(): lax.all_to_all(requests_grid, 'dp', split_axis=0, concat_axis=0, tiled=True)  16.6 us
    all_to_all x1, waiting for transfers between devices, on_device(): lax.all_to_all(found_rows, 'dp', split_axis=0, concat_axis=0, tiled=True)  15.7 us
    all_gather x1, blocking collectives, on_device(): lax.all_gather(neighbour_mean, 'feat', axis=1, tiled=True)  14.1 us
    all_gather x1, blocking collectives, on_device(): lax.all_gather(self_rows, 'feat', axis=1, tiled=True)  13.5 us
    another operation x1, loops' own time, on_device(): summed, degree = lax.fori_loop(0, tile_count[0], add_tile, start_state)  12.6 us
    all_to_all x1, waiting for transfers between devices, on_device(): lax.all_to_all(requests_grid, 'dp', split_axis=0, concat_axis=0, tiled=True)  10.8 us
  transfers between devices with their start and end apart: 7, of which 5 were waited for; matrix products, arithmetic and copies ran while one was open for 8% of the time, Pallas kernels for 0%

commit v1 on v0

v1 whole, which is shorter than its diff:
```python
import jax
import jax.numpy as jnp
from jax import lax
from jax.experimental import pallas as pl
from jax.experimental.pallas import tpu as pltpu
from jax.sharding import PartitionSpec as P

MESH = pl.DeviceIdType.MESH
F32 = jnp.float32
BF16 = jnp.bfloat16
NY, NZ, NX, NF = 8, 8, 4, 8
NDP = NY * NZ
BLK = 128
LANES = 128
TILE = 16


def dot(a, b):
    return jnp.dot(a, b, preferred_element_type=F32)


def kernel(
    table_hbm, ids_hbm, tiles_hbm, rows_s, cols_s, count_s, seed_s, ws_hbm, wn_hbm, bias_ref, cot_hbm,
    hidden_ref, gself_ref, gneigh_ref, gbias_ref,
    table_f, table_b, tiles_i, tiles_f, ws_f, wn_f, w_b, cot_v,
    ids_buf, rows_send, rows_buf, adj, x_b, xt_b,
    p_send, p_recv, p_own, sl_all,
    s1_send, s1_recv, n1_send, n1_recv, s1_own, n1_own,
    s2_send, s2_recv, n2_send, n2_recv,
    s3_buf, n3_buf, s4_buf, n4_buf,
    loc_sem, ids_ss, ids_rs, rows_ss, rows_rs, send_sem, send2_sem,
    p_rs, sl_rs, s1_rs, n1_rs, s2_rs, n2_rs, s3_rs, n3_rs, s4_rs, n4_rs,
):
    me = lax.axis_index("dp")
    feat = lax.axis_index("feat")
    y = me // NZ
    z = me % NZ
    x = feat // 2
    core = feat % 2
    fcols = table_f.shape[1]
    targets = cot_v.shape[0]
    s_tiles = s1_send.shape[1] // TILE
    n_tiles = n1_send.shape[1] // TILE

    def dp_of(yy, zz):
        return yy * NZ + zz

    own_ids = pltpu.make_async_copy(ids_hbm.at[y], ids_buf.at[me], loc_sem.at[0])
    get_table = pltpu.make_async_copy(table_hbm, table_f, loc_sem.at[1])
    get_ws = pltpu.make_async_copy(ws_hbm, ws_f, loc_sem.at[2])
    get_wn = pltpu.make_async_copy(wn_hbm, wn_f, loc_sem.at[3])
    get_tiles = pltpu.make_async_copy(tiles_hbm, tiles_i, loc_sem.at[4])
    get_cot = pltpu.make_async_copy(cot_hbm, cot_v, loc_sem.at[5])
    own_ids.start()
    get_table.start()
    get_ws.start()
    get_wn.start()
    get_tiles.start()
    get_cot.start()

    barrier = pltpu.get_barrier_semaphore()

    def greet_dp(k, c):
        pl.semaphore_signal(barrier, inc=1, device_id=((me + k) % NDP, feat), device_id_type=MESH)
        return c

    lax.fori_loop(1, NDP, greet_dp, 0)

    def greet_feat(k, c):
        pl.semaphore_signal(barrier, inc=1, device_id=(me, (feat + k) % NF), device_id_type=MESH)
        return c

    lax.fori_loop(1, NF, greet_feat, 0)
    pl.semaphore_wait(barrier, NDP - 1 + NF - 1)

    def send_ids(k, c):
        yy = (y + k // NZ) % NY
        zz = (z + k % NZ) % NZ
        pltpu.make_async_remote_copy(
            ids_hbm.at[yy], ids_buf.at[me], ids_ss, ids_rs,
            device_id=(dp_of(yy, zz), feat), device_id_type=MESH,
        ).start()
        return c

    lax.fori_loop(1, NDP, send_ids, 0)

    get_table.wait()
    table_b[...] = jnp.zeros_like(table_b)
    table_b[:, :fcols] = table_f[...].astype(BF16)
    own_ids.wait()
    pltpu.make_async_copy(ids_buf.at[pl.ds(0, NDP - 1)], ids_buf.at[pl.ds(0, NDP - 1)], ids_rs).wait()

    lane = lax.broadcasted_iota(jnp.int32, (NZ, TILE, LANES), 2)
    slot = lax.broadcasted_iota(jnp.int32, (NZ, TILE, LANES), 1)
    mine = lane == z * TILE + slot
    table_rows = table_b.shape[0]
    row_of = lax.broadcasted_iota(jnp.int32, (NZ * TILE, table_rows), 1)

    def gather(dy, c):
        yy = (y + dy) % NY
        asked = ids_buf[pl.ds(yy * NZ, NZ)].astype(F32)
        picked = jnp.where(mine, jnp.broadcast_to(asked, (NZ, TILE, LANES)), 0.0)
        column = jnp.sum(picked.reshape(NZ * TILE, LANES), axis=1, keepdims=True).astype(jnp.int32)
        hot = jnp.where(column == row_of, 1.0, 0.0).astype(BF16)
        found = dot(hot, table_b[...]).astype(BF16)
        rows_send[pl.ds(yy * NZ, NZ)] = found.reshape(NZ, TILE, LANES)
        for dz in range(NZ):
            zz = (z + dz) % NZ
            copy = pltpu.make_async_remote_copy(
                rows_send.at[dp_of(yy, zz)], rows_buf.at[me], rows_ss, rows_rs,
                device_id=(dp_of(yy, zz), feat), device_id_type=MESH,
            )
            if dz == 0:
                pl.when(dy > 0)(copy.start)
            else:
                copy.start()
        return c

    lax.fori_loop(0, NY, gather, 0)
    rows_buf[me] = rows_send[me]

    get_ws.wait()
    get_wn.wait()
    w_b[...] = jnp.zeros_like(w_b)
    for c in range(NX):
        w_b[c, :fcols] = ws_f[:, c * 256:(c + 1) * 256].astype(BF16)
        w_b[c, LANES:LANES + fcols] = wn_f[:, c * 256:(c + 1) * 256].astype(BF16)
    get_tiles.wait()
    tiles_f[...] = tiles_i[...].astype(F32)
    n_slots = tiles_f.shape[0]
    col_blocks = adj.shape[1] // BLK

    def place(i, c):
        r = i // col_blocks
        q = i % col_blocks
        total = jnp.zeros((BLK, BLK), F32)
        for k in range(n_slots):
            on = (rows_s[k] == r) & (cols_s[k] == q) & (k < count_s[0])
            total = total + tiles_f[k] * jnp.where(on, 1.0, 0.0)
        adj[pl.ds(pl.multiple_of(r * BLK, BLK), BLK), pl.ds(pl.multiple_of(q * BLK, BLK), BLK)] = total.astype(BF16)
        return c

    lax.fori_loop(0, (targets // BLK) * col_blocks, place, 0)
    degree = jnp.sum(adj[...].astype(F32), axis=1, keepdims=True)
    scale = 1.0 / jnp.maximum(degree, 1.0)
    get_cot.wait()

    pltpu.make_async_copy(rows_buf.at[pl.ds(0, NDP - 1)], rows_buf.at[pl.ds(0, NDP - 1)], rows_rs).wait()
    sampled = rows_buf[...].reshape(NDP * TILE, LANES)
    self_rows = sampled[:targets]
    neigh = dot(adj[...], sampled) * scale
    x_b[:, :LANES] = self_rows
    x_b[:, LANES:] = neigh.astype(BF16)

    def partial(k, c):
        chip = (x + 2 + k) % NX
        part = dot(x_b[...], w_b[chip])
        for co in range(2):
            p_send[chip * 2 + co] = part[:, co * LANES:(co + 1) * LANES].astype(BF16)
            to = chip * 2 + co
            copy = pltpu.make_async_remote_copy(
                p_send.at[to], p_recv.at[feat], send_sem.at[0], p_rs.at[feat],
                device_id=(me, to), device_id_type=MESH,
            )
            pl.when(to != feat)(copy.start)

            @pl.when(to == feat)
            def _():
                p_own[...] = part[:, co * LANES:(co + 1) * LANES]
        return c

    lax.fori_loop(0, NX, partial, 0)

    xs_t = self_rows.astype(F32).T
    xn_t = neigh.T
    ones = jnp.where(lax.broadcasted_iota(jnp.int32, (TILE, targets), 0) == 0, 1.0, 0.0)
    xt_b[:fcols] = xs_t[:fcols].astype(BF16)
    xt_b[fcols:fcols + TILE] = ones.astype(BF16)
    xt_b[fcols + TILE:] = xn_t[:fcols].astype(BF16)

    preact = p_own[...] + bias_ref[...]

    def add_partial(k, total):
        frm = (feat + k) % NF
        pltpu.make_async_copy(p_recv.at[frm], p_recv.at[frm], p_rs.at[frm]).wait()
        return total + p_recv[frm].astype(F32)

    preact = lax.fori_loop(1, NF, add_partial, preact)
    alive = jnp.where(lax.broadcasted_iota(jnp.int32, (targets, LANES), 0) < seed_s[0], 1.0, 0.0)
    sigma = jax.nn.sigmoid(preact)
    slope = cot_v[...].astype(F32) * alive * sigma * (1.0 + preact * (1.0 - sigma))
    sl_all[feat] = slope.astype(BF16)

    def send_slope(k, c):
        to = (feat + k) % NF
        pltpu.make_async_remote_copy(
            sl_all.at[feat], sl_all.at[feat], send_sem.at[1], sl_rs.at[feat],
            device_id=(me, to), device_id_type=MESH,
        ).start()
        return c

    lax.fori_loop(1, NF, send_slope, 0)
    hidden_ref[...] = (preact * sigma * alive).astype(BF16)

    def wait_slope(k, c):
        frm = (feat + k) % NF
        pltpu.make_async_copy(sl_all.at[frm], sl_all.at[frm], sl_rs.at[frm]).wait()
        return c

    lax.fori_loop(1, NF, wait_slope, 0)

    s_rows = s1_send.shape[1]

    def first(k, c):
        cz = (z + k) % NZ
        cy = (y + k) % NY
        g_s = dot(xt_b[:s_rows], sl_all[cz])
        g_n = dot(xt_b[s_rows:], sl_all[cy])
        s1_send[cz] = g_s.astype(BF16)
        n1_send[cy] = g_n.astype(BF16)
        pltpu.make_async_remote_copy(
            s1_send.at[cz], s1_recv.at[z], send_sem.at[2], s1_rs.at[z],
            device_id=(dp_of(y, cz), feat), device_id_type=MESH,
        ).start()
        pltpu.make_async_remote_copy(
            n1_send.at[cy], n1_recv.at[y], send_sem.at[3], n1_rs.at[y],
            device_id=(dp_of(cy, z), feat), device_id_type=MESH,
        ).start()
        return c

    lax.fori_loop(1, NZ, first, 0)
    s1_own[...] = dot(xt_b[:s_rows], sl_all[z])
    n1_own[...] = dot(xt_b[s_rows:], sl_all[y])

    def add_first(k, c):
        fz = (z + k) % NZ
        fy = (y + k) % NY
        pltpu.make_async_copy(s1_recv.at[fz], s1_recv.at[fz], s1_rs.at[fz]).wait()
        s1_own[...] += s1_recv[fz].astype(F32)
        pltpu.make_async_copy(n1_recv.at[fy], n1_recv.at[fy], n1_rs.at[fy]).wait()
        n1_own[...] += n1_recv[fy].astype(F32)
        return c

    lax.fori_loop(1, NZ, add_first, 0)
    s2_send[...] = s1_own[...].reshape(s_tiles, TILE, LANES)
    n2_send[...] = n1_own[...].reshape(n_tiles, TILE, LANES)

    def s2_copy(k):
        to = (y + k) % NY
        return to, pltpu.make_async_remote_copy(
            s2_send.at[lax.min(to, s_tiles - 1)], s2_recv.at[y], send2_sem.at[0, k], s2_rs.at[y],
            device_id=(dp_of(to, z), feat), device_id_type=MESH,
        )

    def n2_copy(k):
        to = (z + k) % NZ
        return to, pltpu.make_async_remote_copy(
            n2_send.at[lax.min(to, n_tiles - 1)], n2_recv.at[z], send2_sem.at[1, k], n2_rs.at[z],
            device_id=(dp_of(y, to), feat), device_id_type=MESH,
        )

    def second(k, c):
        to, copy = s2_copy(k)
        pl.when(to < s_tiles)(copy.start)
        to, copy = n2_copy(k)
        pl.when(to < n_tiles)(copy.start)
        return c

    lax.fori_loop(1, NZ, second, 0)

    def s3_copy(k):
        return pltpu.make_async_remote_copy(
            s3_buf.at[lax.min(y, s_tiles - 1)], s3_buf.at[lax.min(y, s_tiles - 1)], send2_sem.at[2, k], s3_rs.at[y],
            device_id=(dp_of((y + k) % NY, z), feat), device_id_type=MESH,
        )

    def n3_copy(k):
        return pltpu.make_async_remote_copy(
            n3_buf.at[lax.min(z, n_tiles - 1)], n3_buf.at[lax.min(z, n_tiles - 1)], send2_sem.at[3, k], n3_rs.at[z],
            device_id=(dp_of(y, (z + k) % NZ), feat), device_id_type=MESH,
        )

    @pl.when(y < s_tiles)
    def _():
        def add(k, total):
            frm = (y + k) % NY
            pltpu.make_async_copy(s2_recv.at[frm], s2_recv.at[frm], s2_rs.at[frm]).wait()
            return total + s2_recv[frm]

        s3_buf[lax.min(y, s_tiles - 1)] = lax.fori_loop(1, NY, add, s2_send[lax.min(y, s_tiles - 1)]).astype(BF16)

        def send(k, c):
            s3_copy(k).start()
            return c

        lax.fori_loop(1, NY, send, 0)

    @pl.when(z < n_tiles)
    def _():
        def add(k, total):
            frm = (z + k) % NZ
            pltpu.make_async_copy(n2_recv.at[frm], n2_recv.at[frm], n2_rs.at[frm]).wait()
            return total + n2_recv[frm]

        n3_buf[lax.min(z, n_tiles - 1)] = lax.fori_loop(1, NZ, add, n2_send[lax.min(z, n_tiles - 1)]).astype(BF16)

        def send(k, c):
            n3_copy(k).start()
            return c

        lax.fori_loop(1, NZ, send, 0)

    def wait_third(k, c):
        frm = (y + k) % NY
        at = lax.min(frm, s_tiles - 1)

        @pl.when(frm < s_tiles)
        def _():
            pltpu.make_async_copy(s3_buf.at[at], s3_buf.at[at], s3_rs.at[frm]).wait()

        frm2 = (z + k) % NZ
        at2 = lax.min(frm2, n_tiles - 1)

        @pl.when(frm2 < n_tiles)
        def _():
            pltpu.make_async_copy(n3_buf.at[at2], n3_buf.at[at2], n3_rs.at[frm2]).wait()

        return c

    lax.fori_loop(1, NZ, wait_third, 0)
    s4_buf[z] = s3_buf[...].reshape(s_rows, LANES)
    n4_buf[y] = n3_buf[...].reshape(n_tiles * TILE, LANES)

    def fourth(k, c):
        pltpu.make_async_remote_copy(
            s4_buf.at[z], s4_buf.at[z], send_sem.at[4], s4_rs.at[z],
            device_id=(dp_of(y, (z + k) % NZ), feat), device_id_type=MESH,
        ).start()
        pltpu.make_async_remote_copy(
            n4_buf.at[y], n4_buf.at[y], send_sem.at[5], n4_rs.at[y],
            device_id=(dp_of((y + k) % NY, z), feat), device_id_type=MESH,
        ).start()
        return c

    lax.fori_loop(1, NZ, fourth, 0)

    def wait_fourth(k, c):
        fz = (z + k) % NZ
        fy = (y + k) % NY
        pltpu.make_async_copy(s4_buf.at[fz], s4_buf.at[fz], s4_rs.at[fz]).wait()
        pltpu.make_async_copy(n4_buf.at[fy], n4_buf.at[fy], n4_rs.at[fy]).wait()
        return c

    lax.fori_loop(1, NZ, wait_fourth, 0)
    for c in range(NF):
        gself_ref[:, c * LANES:(c + 1) * LANES] = s4_buf[c][:fcols].astype(F32)
        gneigh_ref[:, c * LANES:(c + 1) * LANES] = n4_buf[c].astype(F32)
    gbias_ref[...] = s4_buf[feat][fcols:fcols + TILE].astype(F32)[:1]

    def sent(buf, count, sem):
        pltpu.make_async_copy(buf.at[pl.ds(0, count)], buf.at[pl.ds(0, count)], sem).wait()

    sent(ids_buf, NDP - 1, ids_ss)
    sent(rows_send, NDP - 1, rows_ss)
    sent(p_send, NF - 1, send_sem.at[0])
    sent(sl_all, NF - 1, send_sem.at[1])
    sent(s1_send, NZ - 1, send_sem.at[2])
    sent(n1_send, NY - 1, send_sem.at[3])
    sent(s4_buf, NZ - 1, send_sem.at[4])
    sent(n4_buf, NY - 1, send_sem.at[5])

    def left(k, c):
        to, copy = s2_copy(k)
        pl.when(to < s_tiles)(copy.wait_send)
        to, copy = n2_copy(k)
        pl.when(to < n_tiles)(copy.wait_send)
        pl.when(y < s_tiles)(s3_copy(k).wait_send)
        pl.when(z < n_tiles)(n3_copy(k).wait_send)
        return c

    lax.fori_loop(1, NZ, left, 0)


def on_device(table, node_ids, tiles, tile_rows, tile_cols, tile_count, seed_count, w_self, w_neigh, bias, cotangent):
    fcols = table.shape[1]
    hidden_all = w_self.shape[1]
    targets, hid = cotangent.shape
    s_rows, n_rows = fcols + TILE, fcols
    vmem = pltpu.VMEM
    dma = pltpu.SemaphoreType.DMA
    hbm = pl.BlockSpec(memory_space=pl.ANY)
    in_vmem = pl.BlockSpec(memory_space=pltpu.VMEM)
    smem = pl.BlockSpec(memory_space=pltpu.SMEM)
    scratch = [
        vmem(table.shape, F32),
        vmem((table.shape[0], LANES), BF16),
        vmem(tiles.shape, jnp.int32),
        vmem(tiles.shape, F32),
        vmem(w_self.shape, F32),
        vmem(w_neigh.shape, F32),
        vmem((NX, 2 * LANES, hidden_all // NX), BF16),
        vmem(cotangent.shape, BF16),
        vmem((NDP, 1, LANES), jnp.int32),
        vmem((NDP, TILE, LANES), BF16),
        vmem((NDP, TILE, LANES), BF16),
        vmem((targets, NDP * TILE), BF16),
        vmem((targets, 2 * LANES), BF16),
        vmem((s_rows + n_rows, targets), BF16),
        vmem((NF, targets, hid), BF16),
        vmem((NF, targets, hid), BF16),
        vmem((targets, hid), F32),
        vmem((NF, targets, hid), BF16),
        vmem((NZ, s_rows, LANES), BF16),
        vmem((NZ, s_rows, LANES), BF16),
        vmem((NY, n_rows, LANES), BF16),
        vmem((NY, n_rows, LANES), BF16),
        vmem((s_rows, LANES), F32),
        vmem((n_rows, LANES), F32),
        vmem((s_rows // TILE, TILE, LANES), F32),
        vmem((NY, TILE, LANES), F32),
        vmem((n_rows // TILE, TILE, LANES), F32),
        vmem((NZ, TILE, LANES), F32),
        vmem((s_rows // TILE, TILE, LANES), BF16),
        vmem((n_rows // TILE, TILE, LANES), BF16),
        vmem((NZ, s_rows, LANES), BF16),
        vmem((NY, n_rows, LANES), BF16),
        dma((6,)),
        dma, dma, dma, dma,
        dma((6,)),
        dma((4, NZ)),
    ] + [dma((8,))] * 10
    hidden, grad_self, grad_neigh, grad_bias = pl.pallas_call(
        kernel,
        out_shape=(
            jax.ShapeDtypeStruct((targets, hid), BF16),
            jax.ShapeDtypeStruct(w_self.shape, F32),
            jax.ShapeDtypeStruct(w_neigh.shape, F32),
            jax.ShapeDtypeStruct((1, hid), F32),
        ),
        in_specs=[hbm, hbm, hbm, smem, smem, smem, smem, hbm, hbm, in_vmem, hbm],
        out_specs=(in_vmem,) * 4,
        scratch_shapes=scratch,
        compiler_params=pltpu.CompilerParams(
            collective_id=0, has_side_effects=True, vmem_limit_bytes=40 * 1024 * 1024
        ),
        cost_estimate=pl.CostEstimate(flops=300_000_000, bytes_accessed=4_000_000, transcendentals=65536),
    )(
        table, node_ids.reshape(NY, 1, NZ * TILE), tiles, tile_rows, tile_cols, tile_count, seed_count,
        w_self, w_neigh, bias.reshape(1, hid), cotangent,
    )
    return hidden, grad_self, grad_neigh, grad_bias.reshape(hid)


def solution(mesh):
    placed = (
        P("dp", "feat"),
        P("dp"),
        P("dp", None, None),
        P("dp"),
        P("dp"),
        P("dp"),
        P("dp"),
        P("feat", None),
        P("feat", None),
        P("feat"),
        P("dp", "feat"),
    )
    return jax.shard_map(
        on_device,
        mesh=mesh,
        in_specs=placed,
        out_specs=(P("dp", "feat"), P("feat", None), P("feat", None), P("feat")),
        check_vma=False,
    )
```

time: 340 us -> 84.1 us (0.25)
  blocking collectives: 173 us -> 0 us
  Pallas kernels: 0 us -> 75.5 us
  waiting for transfers between devices: 55.9 us -> 0 us
  starting transfers between devices: 41 us -> 0 us
  local copies, waits for them, and re-layouts: 21.1 us -> 5.78 us
  between operations: 14.8 us -> 2.1 us
  matrix products: 12.6 us -> 0 us
  loops' own time: 12.6 us -> 0 us
  other arithmetic: 6.74 us -> 0 us
    psum x1 -> x0, blocking collectives: 146 us -> none  [on_device(): lax.psum((grad_self, grad_neigh, grad_bias), 'dp')]
    pallas_call x0 -> x1, Pallas kernels: none -> 75.5 us  [on_device(): pl.pallas_call(kernel, out_shape=(jax.ShapeDtypeStruct((targets, hid), BF...]
    all_to_all x6 -> x0, starting transfers between devices: 41 us -> none  [the longest x1 16.6 us: on_device(): lax.all_to_all(requests_grid, 'dp', split_axis=0, concat_axis=0, tiled=True)]
    all_to_all x6 -> x0, waiting for transfers between devices: 38.3 us -> none  [the longest x1 15.7 us: on_device(): lax.all_to_all(found_rows, 'dp', split_axis=0, concat_axis=0, tiled=True)]
    all_gather x2 -> x0, blocking collectives: 27.6 us -> none  [the longest x1 14.1 us: on_device(): lax.all_gather(neighbour_mean, 'feat', axis=1, tiled=True)]
    psum x1 -> x0, waiting for transfers between devices: 17.6 us -> none  [on_device(): lax.psum((grad_self, grad_neigh, grad_bias), 'dp')]
    dot_general x10 -> x0, matrix products: 12.6 us -> none  [the longest x6 6.72 us: add_tile(): product = jnp.dot(tile_block, sources, precision=highest)]
    another operation x1 -> x0, loops' own time: 12.6 us -> none  [on_device(): summed, degree = lax.fori_loop(0, tile_count[0], add_tile, start_state)]
  transfers between devices with their start and end apart: 7 -> 0, of which waited for: 5 -> 0; matrix products, arithmetic and copies ran while one was open for 8% -> 0% of each run, Pallas kernels for 0% -> 0%
where the time goes in v1:
time: 84.1 us; the launch traced here: 83.4 us
  Pallas kernels  75.5 us (90%)
  local copies, waits for them, and re-layouts  5.78 us (7%)
  between operations  2.1 us (2%)
    pallas_call x1, Pallas kernels, on_device(): pl.pallas_call(kernel, out_shape=(jax.ShapeDtypeStruct((targets, hid), BF...  75.5 us
    unnamed x21, local copies, waits for them, and re-layouts  5.78 us

profile of v1, /device:TPU:6, one launch (start us, length us, event | category | flops | bytes accessed | tf_op | source)
XLA Modules:
  0.0 83.4 jit_solution(18161055556660030572)
XLA Ops:
  0.6 0.0 copy-start.1
  2.0 0.0 copy-start.3
  2.0 0.0 copy-start.4
  2.0 0.0 copy-start.5
  2.0 0.0 copy-start.6
  2.0 0.0 copy-start.7
  2.0 1.1 %copy.15.table_hbm = f32[512,96]{1,0:T(8,128)S(1)} copy(f32[512,96]{0,1:T(8,128)} %param.11) | data formatting | bytes 393216 | tf_op args[0]
  3.1 0.0 copy-done.1
  3.1 0.0 copy-done.3
  3.2 0.0 copy-done.4
  3.2 0.0 copy-done.5
  3.2 0.0 copy-done.6
  3.2 0.0 copy-done.7
  3.2 0.0 copy-start
  3.2 1.0 %copy-done = s32[8,128,128]{2,1,0:T(8,128)S(1)} copy-done((s32[8,128,128]{2,1,0:T(8,128)S(1)}, s32[8,128,128]{2,1,0:T(8,128)}, u32[]{:S(2)}) %copy-start) | copy-done | bytes 524312
  4.2 0.0 copy-start.2
  4.2 1.0 %copy-done.2 = f32[96,1024]{1,0:T(8,128)S(1)} copy-done((f32[96,1024]{1,0:T(8,128)S(1)}, f32[96,1024]{1,0:T(8,128)}, u32[]{:S(2)}) %copy-start.2) | copy-done | bytes 393240
  5.2 75.5 %shard_map.138 = (bf16[256,128]{1,0:T(8,128)(2,1)S(1)}, f32[96,1024]{1,0:T(8,128)S(1)}, f32[96,1024]{1,0:T(8,128)S(1)}, f32[1,128]{1,0:T(1,128)S(1)}) custom-call(f32[512,96]{1,0:T(8,128)S(1)} %copy.15.table_hbm, s32[8,1,128]{2,1,0:T(1,128)S(1)} %bitcast.3, s32[8,128,128]{2,1,0:T(8,128)S(1)} %copy-done, s32[8]{0:T(128)S(1)} %copy-done.5, s32[8]{0:T(128)S(1)} %copy-done.6, ...), custom_call_target="tpu_custom_call" | custom-call | flops 300000000 | bytes 4000000 | tf_op jit(solution)/shard_map/pallas_call | solution.py:432
  80.8 0.6 copy.22
  81.4 0.7 copy.23
  82.1 0.7 copy.24
  82.9 0.5 copy.25
Async XLA Ops:
  0.6 2.5 %copy-start.1 = (f32[96,1024]{1,0:T(8,128)S(1)}, f32[96,1024]{1,0:T(8,128)}, u32[]{:S(2)}) copy-start(f32[96,1024]{1,0:T(8,128)} %ws_hbm.1) | copy-start | bytes 1179652
  2.0 1.2 %copy-start.3 = (bf16[256,128]{1,0:T(8,128)(2,1)S(1)}, bf16[256,128]{1,0:T(8,128)(2,1)}, u32[]{:S(2)}) copy-start(bf16[256,128]{1,0:T(8,128)(2,1)} %cot_hbm.1) | copy-start | bytes 196612
  2.0 1.2 %copy-start.4 = (s32[1024]{0:T(1024)S(1)}, s32[1024]{0:T(1024)}, u32[]{:S(2)}) copy-start(s32[1024]{0:T(1024)} %param.12) | copy-start | bytes 12292
  2.0 1.2 %copy-start.5 = (s32[8]{0:T(128)S(1)}, s32[8]{0:T(128)}, u32[]{:S(2)}) copy-start(s32[8]{0:T(128)} %rows_s.1) | copy-start | bytes 100
  2.0 1.2 %copy-start.6 = (s32[8]{0:T(128)S(1)}, s32[8]{0:T(128)}, u32[]{:S(2)}) copy-start(s32[8]{0:T(128)} %cols_s.1) | copy-start | bytes 100
  2.0 1.2 %copy-start.7 = (f32[128]{0:T(128)S(1)}, f32[128]{0:T(128)}, u32[]{:S(2)}) copy-start(f32[128]{0:T(128)} %param.20) | copy-start | bytes 1540
  3.2 1.0 %copy-start = (s32[8,128,128]{2,1,0:T(8,128)S(1)}, s32[8,128,128]{2,1,0:T(8,128)}, u32[]{:S(2)}) copy-start(s32[8,128,128]{2,1,0:T(8,128)} %tiles_hbm.1) | copy-start | bytes 1572868
  4.2 1.0 %copy-start.2 = (f32[96,1024]{1,0:T(8,128)S(1)}, f32[96,1024]{1,0:T(8,128)}, u32[]{:S(2)}) copy-start(f32[96,1024]{1,0:T(8,128)} %wn_hbm.1) | copy-start | bytes 1179652

commit v2 on v1

v2 whole, which is shorter than its diff:
```python
import jax
import jax.numpy as jnp
from jax import lax
from jax.experimental import pallas as pl
from jax.experimental.pallas import tpu as pltpu
from jax.sharding import PartitionSpec as P

MESH = pl.DeviceIdType.MESH
F32 = jnp.float32
BF16 = jnp.bfloat16
NY, NZ, NX, NF = 8, 8, 4, 8
NDP = NY * NZ
BLK = 128
LANES = 128
VMEM_LIMIT = 60 * 1024 * 1024
TILE = 16


RING = (4, 5, 3, 6, 2, 7, 1)
CHIPS = (2, 1, 3)


def dot(a, b):
    return jnp.dot(a, b, preferred_element_type=F32)


def dot_t(a, b):
    return lax.dot_general(a, b, (((1,), (1,)), ((), ())), preferred_element_type=F32)


def kernel(
    table_hbm, ids_hbm, tiles_hbm, rows_s, cols_s, count_s, seed_s, ws_hbm, wn_hbm, bias_ref, cot_hbm,
    hidden_ref, s4_buf, n4_buf,
    table_f, table_b, tiles_i, tiles_f, ws_f, wn_f, w_b, cot_v,
    ids_y, ids_buf, rows_send, rows_buf, adj, x_b, xt_b,
    q_send, q_recv, q_own, p_send, p_recv, sl_all,
    s1_send, s1_recv, n1_send, n1_recv, s1_own, n1_own,
    s2_send, s2_recv, n2_send, n2_recv,
    s3_buf, n3_buf,
    loc_sem, ids_ss, idy_rs, idz_rs, rows_ss, rows_rs, q_ss, q_rs, send_sem, send2_sem,
    p_rs, sl_rs, s1_rs, n1_rs, s2_rs, n2_rs, s3_rs, n3_rs, s4_rs, n4_rs,
):
    me = lax.axis_index("dp")
    feat = lax.axis_index("feat")
    y = me // NZ
    z = me % NZ
    x = feat // 2
    core = feat % 2
    fcols = table_f.shape[0]
    mate = x * 2 + 1 - core
    targets = cot_v.shape[0]
    s_tiles = s1_send.shape[1] // TILE
    n_tiles = n1_send.shape[1] // TILE

    def dp_of(yy, zz):
        return yy * NZ + zz

    own_ids = pltpu.make_async_copy(ids_hbm.at[y], ids_y.at[y], loc_sem.at[0])
    get_table = pltpu.make_async_copy(table_hbm, table_f, loc_sem.at[1])
    get_ws = pltpu.make_async_copy(ws_hbm, ws_f, loc_sem.at[2])
    get_wn = pltpu.make_async_copy(wn_hbm, wn_f, loc_sem.at[3])
    get_tiles = pltpu.make_async_copy(tiles_hbm, tiles_i, loc_sem.at[4])
    get_cot = pltpu.make_async_copy(cot_hbm, cot_v, loc_sem.at[5])
    own_ids.start()
    get_table.start()
    get_ws.start()
    get_wn.start()
    get_tiles.start()
    get_cot.start()

    barrier = pltpu.get_barrier_semaphore()

    for k in RING:
        pl.semaphore_signal(barrier, inc=1, device_id=(dp_of((y + k) % NY, z), feat), device_id_type=MESH)
    for k in RING:
        pl.semaphore_signal(barrier, inc=1, device_id=(dp_of(y, (z + k) % NZ), feat), device_id_type=MESH)
    for k in CHIPS:
        pl.semaphore_signal(barrier, inc=1, device_id=(me, (x + k) % NX * 2 + core), device_id_type=MESH)
    pl.semaphore_signal(barrier, inc=1, device_id=(me, mate), device_id_type=MESH)
    pl.semaphore_wait(barrier, NZ - 1 + NY - 1 + NX)

    for k in RING:
        yy = (y + k) % NY
        pltpu.make_async_remote_copy(
            ids_hbm.at[yy], ids_y.at[y], ids_ss.at[0], idy_rs,
            device_id=(dp_of(yy, z), feat), device_id_type=MESH,
        ).start()
    own_ids.wait()
    pltpu.make_async_copy(ids_y.at[pl.ds(0, NY - 1)], ids_y.at[pl.ds(0, NY - 1)], idy_rs).wait()
    for k in RING:
        pltpu.make_async_remote_copy(
            ids_y, ids_buf.at[z], ids_ss.at[1], idz_rs,
            device_id=(dp_of(y, (z + k) % NZ), feat), device_id_type=MESH,
        ).start()
    ids_buf[z] = ids_y[...]

    get_table.wait()
    table_b[...] = table_f[...].astype(BF16)
    pltpu.make_async_copy(ids_buf.at[pl.ds(0, NZ - 1)], ids_buf.at[pl.ds(0, NZ - 1)], idz_rs).wait()

    lane = lax.broadcasted_iota(jnp.int32, (NZ, TILE, LANES), 2)
    slot = lax.broadcasted_iota(jnp.int32, (NZ, TILE, LANES), 1)
    mine = lane == z * TILE + slot
    table_rows = table_b.shape[1]
    row_of = lax.broadcasted_iota(jnp.int32, (NZ * TILE, table_rows), 1)

    def gather(step, c):
        pair = ((y + 4 - step) % NY, (y + 5 + step) % NY)
        for yy in pair:
            asked = ids_buf[:, yy].astype(F32)
            picked = jnp.where(mine, jnp.broadcast_to(asked, (NZ, TILE, LANES)), 0.0)
            column = jnp.sum(picked.reshape(NZ * TILE, LANES), axis=1, keepdims=True).astype(jnp.int32)
            hot = jnp.where(column == row_of, 1.0, 0.0).astype(BF16)
            found = dot_t(hot, table_b[...]).astype(BF16)
            rows_send[pl.ds(yy * NZ, NZ)] = found.reshape(NZ, TILE, fcols)
        for dz in RING + (0,):
            zz = (z + dz) % NZ
            for yy in pair:
                to = dp_of(yy, zz)
                copy = pltpu.make_async_remote_copy(
                    rows_send.at[to], rows_buf.at[me], rows_ss, rows_rs,
                    device_id=(to, feat), device_id_type=MESH,
                )
                if dz == 0:
                    pl.when(to != me)(copy.start)
                else:
                    copy.start()
        return c

    lax.fori_loop(0, NY // 2, gather, 0)
    rows_buf[me] = rows_send[me]

    get_ws.wait()
    get_wn.wait()
    w_b[...] = jnp.zeros_like(w_b)
    x_b[...] = jnp.zeros_like(x_b)
    for c in range(NX):
        for co in range(2):
            at = (c * 2 + co) * LANES
            w_b[c, co, :fcols] = ws_f[:, at:at + LANES].astype(BF16)
            w_b[c, co, LANES:LANES + fcols] = wn_f[:, at:at + LANES].astype(BF16)
    get_tiles.wait()
    tiles_f[...] = tiles_i[...].astype(F32)
    n_slots = tiles_f.shape[0]
    col_blocks = adj.shape[1] // BLK

    def place(i, c):
        r = i // col_blocks
        q = i % col_blocks
        total = jnp.zeros((BLK, BLK), F32)
        for k in range(n_slots):
            on = (rows_s[k] == r) & (cols_s[k] == q) & (k < count_s[0])
            total = total + tiles_f[k] * jnp.where(on, 1.0, 0.0)
        adj[pl.ds(pl.multiple_of(r * BLK, BLK), BLK), pl.ds(pl.multiple_of(q * BLK, BLK), BLK)] = total.astype(BF16)
        return c

    lax.fori_loop(0, (targets // BLK) * col_blocks, place, 0)
    degree = jnp.sum(adj[...].astype(F32), axis=1, keepdims=True)
    scale = 1.0 / jnp.maximum(degree, 1.0)
    get_cot.wait()

    pltpu.make_async_copy(rows_buf.at[pl.ds(0, NDP - 1)], rows_buf.at[pl.ds(0, NDP - 1)], rows_rs).wait()
    sampled = rows_buf[...].reshape(NDP * TILE, fcols)
    self_rows = sampled[:targets]
    neigh = dot(adj[...], sampled) * scale
    x_b[:, :fcols] = self_rows
    x_b[:, LANES:LANES + fcols] = neigh.astype(BF16)

    def pair_copy(chip):
        return pltpu.make_async_remote_copy(
            q_send.at[chip], q_recv.at[chip], q_ss.at[chip], q_rs.at[chip],
            device_id=(me, mate), device_id_type=MESH,
        )

    for k in CHIPS + (0,):
        chip = (x + k) % NX
        q_send[chip] = dot(x_b[...], w_b[chip, 1 - core]).astype(BF16)
        pair_copy(chip).start()
    for k in CHIPS + (0,):
        chip = (x + k) % NX
        q_own[chip] = dot(x_b[...], w_b[chip, core])
    for k in CHIPS:
        chip = (x + k) % NX
        pair_copy(chip).wait_recv()
        p_send[chip] = (q_own[chip] + q_recv[chip].astype(F32)).astype(BF16)
        pltpu.make_async_remote_copy(
            p_send.at[chip], p_recv.at[x], send_sem.at[0], p_rs.at[x],
            device_id=(me, chip * 2 + core), device_id_type=MESH,
        ).start()
    pair_copy(x).wait_recv()
    preact = q_own[x] + q_recv[x].astype(F32) + bias_ref[...]

    xs_t = self_rows.astype(F32).T
    xn_t = neigh.T
    ones = jnp.where(lax.broadcasted_iota(jnp.int32, (TILE, targets), 0) == 0, 1.0, 0.0)
    xt_b[:fcols] = xs_t.astype(BF16)
    xt_b[fcols:fcols + TILE] = ones.astype(BF16)
    xt_b[fcols + TILE:] = xn_t.astype(BF16)

    for k in (1, 3, 2):
        frm = (x + k) % NX
        pltpu.make_async_copy(p_recv.at[frm], p_recv.at[frm], p_rs.at[frm]).wait()
        preact = preact + p_recv[frm].astype(F32)
    alive = jnp.where(lax.broadcasted_iota(jnp.int32, (targets, LANES), 0) < seed_s[0], 1.0, 0.0)
    sigma = jax.nn.sigmoid(preact)
    slope = cot_v[...].astype(F32) * alive * sigma * (1.0 + preact * (1.0 - sigma))
    sl_all[feat] = slope.astype(BF16)

    def slope_copy(which, sem, to):
        return pltpu.make_async_remote_copy(
            sl_all.at[which], sl_all.at[which], sem, sl_rs.at[which],
            device_id=(me, to), device_id_type=MESH,
        )

    for k in CHIPS:
        slope_copy(feat, send_sem.at[1], (x + k) % NX * 2 + core).start()
    slope_copy(feat, q_ss.at[NX], mate).start()
    hidden_ref[...] = (preact * sigma * alive).astype(BF16)

    s_rows = s1_send.shape[1]

    def first(block):
        at = block // 2 + block % 2 * NX
        g_s = dot(xt_b[:s_rows], sl_all[block])
        g_n = dot(xt_b[s_rows:], sl_all[block])

        @pl.when(at == z)
        def _():
            s1_own[...] = g_s

        @pl.when(at == y)
        def _():
            n1_own[...] = g_n

        @pl.when(at != z)
        def _():
            s1_send[at] = g_s.astype(BF16)
            pltpu.make_async_remote_copy(
                s1_send.at[at], s1_recv.at[z], send_sem.at[2], s1_rs.at[z],
                device_id=(dp_of(y, at), feat), device_id_type=MESH,
            ).start()

        @pl.when(at != y)
        def _():
            n1_send[at] = g_n.astype(BF16)
            pltpu.make_async_remote_copy(
                n1_send.at[at], n1_recv.at[y], send_sem.at[3], n1_rs.at[y],
                device_id=(dp_of(at, z), feat), device_id_type=MESH,
            ).start()

    def wait_slope(which):
        pltpu.make_async_copy(sl_all.at[which], sl_all.at[which], sl_rs.at[which]).wait()

    first(feat)
    wait_slope(mate)
    first(mate)
    for n, k in enumerate((1, 3, 2)):
        direct = (x + k) % NX * 2 + core
        passed = (x + k) % NX * 2 + 1 - core
        wait_slope(direct)
        slope_copy(direct, q_ss.at[NX + 1 + n], mate).start()
        first(direct)
        wait_slope(passed)
        first(passed)

    def add_first(own, recv, sems, here, count):
        for k in RING:
            frm = (here - k + count) % count
            pltpu.make_async_copy(recv.at[frm], recv.at[frm], sems.at[frm]).wait()
            own[...] += recv[frm].astype(F32)

    def s2_copy(k):
        to = (y + k) % NY
        return to, pltpu.make_async_remote_copy(
            s2_send.at[lax.min(to, s_tiles - 1)], s2_recv.at[y], send2_sem.at[0, k], s2_rs.at[y],
            device_id=(dp_of(to, z), feat), device_id_type=MESH,
        )

    def n2_copy(k):
        to = (z + k) % NZ
        return to, pltpu.make_async_remote_copy(
            n2_send.at[lax.min(to, n_tiles - 1)], n2_recv.at[z], send2_sem.at[1, k], n2_rs.at[z],
            device_id=(dp_of(y, to), feat), device_id_type=MESH,
        )

    def s3_copy(k):
        return pltpu.make_async_remote_copy(
            s3_buf.at[lax.min(y, s_tiles - 1)], s3_buf.at[lax.min(y, s_tiles - 1)], send2_sem.at[2, k], s3_rs.at[y],
            device_id=(dp_of((y + k) % NY, z), feat), device_id_type=MESH,
        )

    def n3_copy(k):
        return pltpu.make_async_remote_copy(
            n3_buf.at[lax.min(z, n_tiles - 1)], n3_buf.at[lax.min(z, n_tiles - 1)], send2_sem.at[3, k], n3_rs.at[z],
            device_id=(dp_of(y, (z + k) % NZ), feat), device_id_type=MESH,
        )

    add_first(s1_own, s1_recv, s1_rs, z, NZ)
    s2_send[...] = s1_own[...].reshape(s_tiles, TILE, LANES)
    for k in RING:
        to, copy = s2_copy(k)
        pl.when(to < s_tiles)(copy.start)
    add_first(n1_own, n1_recv, n1_rs, y, NY)
    n2_send[...] = n1_own[...].reshape(n_tiles, TILE, LANES)
    for k in RING:
        to, copy = n2_copy(k)
        pl.when(to < n_tiles)(copy.start)

    @pl.when(y < s_tiles)
    def _():
        total = s2_send[lax.min(y, s_tiles - 1)]
        for k in RING:
            frm = (y - k + NY) % NY
            pltpu.make_async_copy(s2_recv.at[frm], s2_recv.at[frm], s2_rs.at[frm]).wait()
            total = total + s2_recv[frm]
        s3_buf[lax.min(y, s_tiles - 1)] = total.astype(BF16)
        for k in RING:
            s3_copy(k).start()

    @pl.when(z < n_tiles)
    def _():
        total = n2_send[lax.min(z, n_tiles - 1)]
        for k in RING:
            frm = (z - k + NZ) % NZ
            pltpu.make_async_copy(n2_recv.at[frm], n2_recv.at[frm], n2_rs.at[frm]).wait()
            total = total + n2_recv[frm]
        n3_buf[lax.min(z, n_tiles - 1)] = total.astype(BF16)
        for k in RING:
            n3_copy(k).start()

    for k in RING:
        frm = (y - k + NY) % NY
        at = lax.min(frm, s_tiles - 1)
        pl.when(frm < s_tiles)(pltpu.make_async_copy(s3_buf.at[at], s3_buf.at[at], s3_rs.at[frm]).wait)
    s4_buf[z] = s3_buf[...].reshape(s_rows, LANES)
    for k in RING:
        pltpu.make_async_remote_copy(
            s4_buf.at[z], s4_buf.at[z], send_sem.at[4], s4_rs.at[z],
            device_id=(dp_of(y, (z + k) % NZ), feat), device_id_type=MESH,
        ).start()
    for k in RING:
        frm = (z - k + NZ) % NZ
        at = lax.min(frm, n_tiles - 1)
        pl.when(frm < n_tiles)(pltpu.make_async_copy(n3_buf.at[at], n3_buf.at[at], n3_rs.at[frm]).wait)
    n4_buf[y] = n3_buf[...].reshape(n_tiles * TILE, LANES)
    for k in RING:
        pltpu.make_async_remote_copy(
            n4_buf.at[y], n4_buf.at[y], send_sem.at[5], n4_rs.at[y],
            device_id=(dp_of((y + k) % NY, z), feat), device_id_type=MESH,
        ).start()
    for k in RING:
        fz = (z + k) % NZ
        fy = (y + k) % NY
        pltpu.make_async_copy(s4_buf.at[fz], s4_buf.at[fz], s4_rs.at[fz]).wait()
        pltpu.make_async_copy(n4_buf.at[fy], n4_buf.at[fy], n4_rs.at[fy]).wait()

    def sent(buf, count, sem):
        pltpu.make_async_copy(buf.at[pl.ds(0, count)], buf.at[pl.ds(0, count)], sem).wait()

    sent(ids_y, NY - 1, ids_ss.at[0])
    sent(ids_buf, NZ - 1, ids_ss.at[1])
    sent(rows_send, NDP - 1, rows_ss)
    sent(p_send, NX - 1, send_sem.at[0])
    sent(sl_all, NX - 1, send_sem.at[1])
    sent(s1_send, NZ - 1, send_sem.at[2])
    sent(n1_send, NY - 1, send_sem.at[3])
    sent(s4_buf, NZ - 1, send_sem.at[4])
    sent(n4_buf, NY - 1, send_sem.at[5])
    for c in range(NX):
        sent(q_send, 1, q_ss.at[c])
        sent(sl_all, 1, q_ss.at[NX + c])
    for k in RING:
        to, copy = s2_copy(k)
        pl.when(to < s_tiles)(copy.wait_send)
        to, copy = n2_copy(k)
        pl.when(to < n_tiles)(copy.wait_send)
        pl.when(y < s_tiles)(s3_copy(k).wait_send)
        pl.when(z < n_tiles)(n3_copy(k).wait_send)


def finish(hidden_in, s4_in, n4_in, hidden_ref, gself_ref, gneigh_ref, gbias_ref, gs_v, gn_v, gb_v, sem):
    fcols = gs_v.shape[0]
    copies = [pltpu.make_async_copy(hidden_in, hidden_ref, sem.at[0])]
    copies[0].start()
    for t in range(NF):
        c = (t % NX) * 2 + t // NX
        gs_v[:, c * LANES:(c + 1) * LANES] = s4_in[t][:fcols].astype(F32)
    copies.append(pltpu.make_async_copy(gs_v, gself_ref, sem.at[1]))
    copies[1].start()
    for t in range(NF):
        c = (t % NX) * 2 + t // NX
        gn_v[:, c * LANES:(c + 1) * LANES] = n4_in[t].astype(F32)
    copies.append(pltpu.make_async_copy(gn_v, gneigh_ref, sem.at[2]))
    copies[2].start()
    feat = lax.axis_index("feat")
    gb_v[...] = s4_in[feat // 2 + feat % 2 * NX][fcols:fcols + TILE].astype(F32)[:1]
    copies.append(pltpu.make_async_copy(gb_v, gbias_ref, sem.at[3]))
    copies[3].start()
    for copy in copies:
        copy.wait()


def on_device(table, node_ids, tiles, tile_rows, tile_cols, tile_count, seed_count, w_self, w_neigh, bias, cotangent):
    fcols = table.shape[1]
    hidden_all = w_self.shape[1]
    targets, hid = cotangent.shape
    s_rows, n_rows = fcols + TILE, fcols
    vmem = pltpu.VMEM
    dma = pltpu.SemaphoreType.DMA
    hbm = pl.BlockSpec(memory_space=pl.ANY)
    in_vmem = pl.BlockSpec(memory_space=pltpu.VMEM)
    smem = pl.BlockSpec(memory_space=pltpu.SMEM)
    scratch = [
        vmem(table.shape[::-1], F32),
        vmem(table.shape[::-1], BF16),
        vmem(tiles.shape, jnp.int32),
        vmem(tiles.shape, F32),
        vmem(w_self.shape, F32),
        vmem(w_neigh.shape, F32),
        vmem((NX, 2, 2 * LANES, LANES), BF16),
        vmem(cotangent.shape, BF16),
        vmem((NY, 1, LANES), jnp.int32),
        vmem((NZ, NY, 1, LANES), jnp.int32),
        vmem((NDP, TILE, fcols), BF16),
        vmem((NDP, TILE, fcols), BF16),
        vmem((targets, NDP * TILE), BF16),
        vmem((targets, 2 * LANES), BF16),
        vmem((s_rows + n_rows, targets), BF16),
        vmem((NX, targets, hid), BF16),
        vmem((NX, targets, hid), BF16),
        vmem((NX, targets, hid), F32),
        vmem((NX, targets, hid), BF16),
        vmem((NX, targets, hid), BF16),
        vmem((NF, targets, hid), BF16),
        vmem((NZ, s_rows, LANES), BF16),
        vmem((NZ, s_rows, LANES), BF16),
        vmem((NY, n_rows, LANES), BF16),
        vmem((NY, n_rows, LANES), BF16),
        vmem((s_rows, LANES), F32),
        vmem((n_rows, LANES), F32),
        vmem((s_rows // TILE, TILE, LANES), F32),
        vmem((NY, TILE, LANES), F32),
        vmem((n_rows // TILE, TILE, LANES), F32),
        vmem((NZ, TILE, LANES), F32),
        vmem((s_rows // TILE, TILE, LANES), BF16),
        vmem((n_rows // TILE, TILE, LANES), BF16),
        dma((6,)),
        dma((2,)), dma, dma, dma, dma,
        dma((2 * NX,)), dma((NX,)),
        dma((6,)),
        dma((4, NZ)),
    ] + [dma((8,))] * 10
    hidden, s4, n4 = pl.pallas_call(
        kernel,
        out_shape=(
            jax.ShapeDtypeStruct((targets, hid), BF16),
            jax.ShapeDtypeStruct((NZ, s_rows, LANES), BF16),
            jax.ShapeDtypeStruct((NY, n_rows, LANES), BF16),
        ),
        in_specs=[hbm, hbm, hbm, smem, smem, smem, smem, hbm, hbm, in_vmem, hbm],
        out_specs=(in_vmem,) * 3,
        scratch_shapes=scratch,
        compiler_params=pltpu.CompilerParams(
            collective_id=0, has_side_effects=True, vmem_limit_bytes=VMEM_LIMIT
        ),
        cost_estimate=pl.CostEstimate(flops=300_000_000, bytes_accessed=4_000_000, transcendentals=65536),
    )(
        table.T, node_ids.reshape(NY, 1, NZ * TILE), tiles, tile_rows, tile_cols,
        tile_count, seed_count, w_self, w_neigh, bias.reshape(1, hid), cotangent,
    )
    hidden, grad_self, grad_neigh, grad_bias = pl.pallas_call(
        finish,
        out_shape=(
            jax.ShapeDtypeStruct((targets, hid), BF16),
            jax.ShapeDtypeStruct(w_self.shape, F32),
            jax.ShapeDtypeStruct(w_neigh.shape, F32),
            jax.ShapeDtypeStruct((1, hid), F32),
        ),
        in_specs=[in_vmem] * 3,
        out_specs=(hbm,) * 4,
        scratch_shapes=[vmem(w_self.shape, F32), vmem(w_neigh.shape, F32), vmem((1, hid), F32), dma((4,))],
    )(hidden, s4, n4)
    return hidden, grad_self, grad_neigh, grad_bias.reshape(hid)


def solution(mesh):
    placed = (
        P("dp", "feat"),
        P("dp"),
        P("dp", None, None),
        P("dp"),
        P("dp"),
        P("dp"),
        P("dp"),
        P("feat", None),
        P("feat", None),
        P("feat"),
        P("dp", "feat"),
    )
    return jax.shard_map(
        on_device,
        mesh=mesh,
        in_specs=placed,
        out_specs=(P("dp", "feat"), P("feat", None), P("feat", None), P("feat")),
        check_vma=False,
    )
```

time: 84.1 us -> 73.7 us (0.88)
  local copies, waits for them, and re-layouts: 5.78 us -> 0 us
  Pallas kernels: 75.5 us -> 71.6 us
    pallas_call x1, Pallas kernels: 75.5 us -> 69.5 us  [on_device(): pl.pallas_call(kernel, out_shape=(jax.ShapeDtypeStruct((targets, hid), BF...]
    unnamed x21 -> x0, local copies, waits for them, and re-layouts: 5.78 us -> none
    pallas_call x0 -> x1, Pallas kernels: none -> 2.02 us  [on_device(): pl.pallas_call(finish, out_shape=(jax.ShapeDtypeStruct((targets, hid), BF...]
where the time goes in v2:
time: 73.7 us; the launch traced here: 73.5 us
  Pallas kernels  71.6 us (97%)
  between operations  1.93 us (3%)
    pallas_call x1, Pallas kernels, on_device(): pl.pallas_call(kernel, out_shape=(jax.ShapeDtypeStruct((targets, hid), BF...  69.5 us
    pallas_call x1, Pallas kernels, on_device(): pl.pallas_call(finish, out_shape=(jax.ShapeDtypeStruct((targets, hid), BF...  2.02 us

profile of v2, /device:TPU:6, one launch (start us, length us, event | category | flops | bytes accessed | tf_op | source)
XLA Modules:
  0.0 73.5 jit_solution(2760492392947981719)
XLA Ops:
  1.9 69.5 %shard_map.138 = (bf16[256,128]{1,0:T(8,128)(2,1)}, bf16[8,112,128]{2,1,0:T(8,128)(2,1)}, bf16[8,96,128]{2,1,0:T(8,128)(2,1)}) custom-call(f32[96,512]{1,0:T(8,128)} %bitcast.4, s32[8,1,128]{2,1,0:T(1,128)} %bitcast.5, s32[8,128,128]{2,1,0:T(8,128)} %tiles_hbm.1, s32[8]{0:T(128)} %rows_s.1, s32[8]{0:T(128)} %cols_s.1, s32[1]{0:T(128)S(6)} %copy.15.count_s, ...), custom_call_target="tpu_custom_call" | custom-call | flops 300000000 | bytes 4000000 | tf_op jit(solution)/shard_map/pallas_call | solution.py:453
  71.5 2.0 %shard_map.139 = (bf16[256,128]{1,0:T(8,128)(2,1)}, f32[96,1024]{1,0:T(8,128)}, f32[96,1024]{1,0:T(8,128)}, f32[1,128]{1,0:T(1,128)}) custom-call(bf16[256,128]{1,0:T(8,128)(2,1)} %get-tuple-element.11.hidden_in, bf16[8,112,128]{2,1,0:T(8,128)(2,1)} %get-tuple-element.12.s4_in, bf16[8,96,128]{2,1,0:T(8,128)(2,1)} %get-tuple-element.13.n4_in), custom_call_target="tpu_custom_call" | custom-call | tf_op jit(solution)/shard_map/pallas_call | solution.py:471

commit v3 on v2

v3 whole, which is shorter than its diff:
```python
import jax
import jax.numpy as jnp
from jax import lax
from jax.experimental import pallas as pl
from jax.experimental.pallas import tpu as pltpu
from jax.sharding import PartitionSpec as P

MESH = pl.DeviceIdType.MESH
F32 = jnp.float32
BF16 = jnp.bfloat16
NY, NZ, NX, NF = 8, 8, 4, 8
NDP = NY * NZ
BLK = 128
LANES = 128
VMEM_LIMIT = 60 * 1024 * 1024
TILE = 16


RING = (4, 5, 3, 6, 2, 7, 1)
CHIPS = (2, 1, 3)
CHUNK_ROWS = ((0, 64, False), (112, 160, True), (64, 112, False), (160, 208, True))
CHUNKS = len(CHUNK_ROWS)


def dot(a, b):
    return jnp.dot(a, b, preferred_element_type=F32)


def dot_t(a, b):
    return lax.dot_general(a, b, (((1,), (1,)), ((), ())), preferred_element_type=F32)


def kernel(
    table_hbm, ids_hbm, tiles_hbm, rows_hbm, cols_hbm, count_hbm, seed_hbm, ws_hbm, wn_hbm, bias_hbm, cot_hbm,
    hidden_hbm, s_hbm, n_hbm,
    table_f, table_b, tiles_i, tiles_f, ws_f, wn_f, w_b, w_p, cot_v, bias_v, rows_s, cols_s, count_s, seed_s,
    ids_y, ids_buf, rows_send, rows_buf, adj, x_b, x_p, xt_b,
    q_own, p_send, p_recv, sl_all, hid_v,
    *rest,
):
    pieces, rest = rest[:5 * CHUNKS], rest[5 * CHUNKS:]
    (
        loc_sem, ids_ss, idy_rs, idz_rs, rows_ss, rows_rs, q_ss, q_rs, send_sem, p_rs, sl_rs, first_rs, second_rs, third_rs,
        out_sem,
    ) = rest
    me = lax.axis_index("dp")
    feat = lax.axis_index("feat")
    y = me // NZ
    z = me % NZ
    x = feat // 2
    core = feat % 2
    fcols = table_f.shape[0]
    mate = x * 2 + 1 - core
    targets = cot_v.shape[0]

    def dp_of(yy, zz):
        return yy * NZ + zz

    own_ids = pltpu.make_async_copy(ids_hbm.at[y], ids_y.at[y], loc_sem.at[0])
    get_table = pltpu.make_async_copy(table_hbm, table_f, loc_sem.at[1])
    get_ws = pltpu.make_async_copy(ws_hbm, ws_f, loc_sem.at[2])
    get_wn = pltpu.make_async_copy(wn_hbm, wn_f, loc_sem.at[3])
    get_tiles = pltpu.make_async_copy(tiles_hbm, tiles_i, loc_sem.at[4])
    get_cot = pltpu.make_async_copy(cot_hbm, cot_v, loc_sem.at[5])
    small = [
        pltpu.make_async_copy(src, dst, loc_sem.at[6 + n])
        for n, (src, dst) in enumerate((
            (rows_hbm, rows_s), (cols_hbm, cols_s), (count_hbm, count_s), (seed_hbm, seed_s), (bias_hbm, bias_v),
        ))
    ]
    own_ids.start()

    barrier = pltpu.get_barrier_semaphore()

    for k in RING:
        pl.semaphore_signal(barrier, inc=1, device_id=(dp_of((y + k) % NY, z), feat), device_id_type=MESH)
    for k in RING:
        pl.semaphore_signal(barrier, inc=1, device_id=(dp_of(y, (z + k) % NZ), feat), device_id_type=MESH)
    for k in CHIPS:
        pl.semaphore_signal(barrier, inc=1, device_id=(me, (x + k) % NX * 2 + core), device_id_type=MESH)
    pl.semaphore_signal(barrier, inc=1, device_id=(me, mate), device_id_type=MESH)
    pl.semaphore_wait(barrier, NZ - 1 + NY - 1 + NX)

    for k in RING:
        yy = (y + k) % NY
        pltpu.make_async_remote_copy(
            ids_hbm.at[yy], ids_y.at[y], ids_ss.at[0], idy_rs,
            device_id=(dp_of(yy, z), feat), device_id_type=MESH,
        ).start()
    get_table.start()
    get_ws.start()
    get_wn.start()
    get_tiles.start()
    for copy in small:
        copy.start()
    get_cot.start()
    own_ids.wait()
    pltpu.make_async_copy(ids_y.at[pl.ds(0, NY - 1)], ids_y.at[pl.ds(0, NY - 1)], idy_rs).wait()
    for k in RING:
        pltpu.make_async_remote_copy(
            ids_y, ids_buf.at[z], ids_ss.at[1], idz_rs,
            device_id=(dp_of(y, (z + k) % NZ), feat), device_id_type=MESH,
        ).start()
    ids_buf[z] = ids_y[...]

    get_table.wait()
    table_b[...] = table_f[...].astype(BF16)
    pltpu.make_async_copy(ids_buf.at[pl.ds(0, NZ - 1)], ids_buf.at[pl.ds(0, NZ - 1)], idz_rs).wait()

    lane = lax.broadcasted_iota(jnp.int32, (NZ, TILE, LANES), 2)
    slot = lax.broadcasted_iota(jnp.int32, (NZ, TILE, LANES), 1)
    mine = lane == z * TILE + slot
    table_rows = table_b.shape[1]
    row_of = lax.broadcasted_iota(jnp.int32, (NZ * TILE, table_rows), 1)

    def gather(step, c):
        pair = ((y + 4 - step) % NY, (y + 5 + step) % NY)
        for yy in pair:
            asked = ids_buf[:, yy].astype(F32)
            picked = jnp.where(mine, jnp.broadcast_to(asked, (NZ, TILE, LANES)), 0.0)
            column = jnp.sum(picked.reshape(NZ * TILE, LANES), axis=1, keepdims=True).astype(jnp.int32)
            hot = jnp.where(column == row_of, 1.0, 0.0).astype(BF16)
            found = dot_t(hot, table_b[...]).astype(BF16)
            rows_send[pl.ds(yy * NZ, NZ)] = found.reshape(NZ, TILE, fcols)
        for dz in RING + (0,):
            zz = (z + dz) % NZ
            for yy in pair:
                to = dp_of(yy, zz)
                copy = pltpu.make_async_remote_copy(
                    rows_send.at[to], rows_buf.at[me], rows_ss, rows_rs,
                    device_id=(to, feat), device_id_type=MESH,
                )
                if dz == 0:
                    pl.when(to != me)(copy.start)
                else:
                    copy.start()
        return c

    lax.fori_loop(0, NY // 2, gather, 0)
    rows_buf[me] = rows_send[me]

    get_ws.wait()
    get_wn.wait()
    w_b[...] = jnp.zeros_like(w_b)
    x_b[...] = jnp.zeros_like(x_b)
    for c in range(NX):
        for co in range(2):
            at = (c * 2 + co) * LANES
            w_b[co, c, :fcols] = ws_f[:, at:at + LANES].astype(BF16)
            w_b[co, c, LANES:LANES + fcols] = wn_f[:, at:at + LANES].astype(BF16)
    w_copy = pltpu.make_async_remote_copy(
        w_b.at[1 - core], w_p, q_ss.at[0], q_rs.at[0], device_id=(me, mate), device_id_type=MESH
    )
    w_copy.start()
    get_tiles.wait()
    tiles_f[...] = tiles_i[...].astype(F32)
    n_slots = tiles_f.shape[0]
    for copy in small:
        copy.wait()
    col_blocks = adj.shape[1] // BLK

    def place(i, c):
        r = i // col_blocks
        q = i % col_blocks
        total = jnp.zeros((BLK, BLK), F32)
        for k in range(n_slots):
            on = (rows_s[k] == r) & (cols_s[k] == q) & (k < count_s[0])
            total = total + tiles_f[k] * jnp.where(on, 1.0, 0.0)
        adj[pl.ds(pl.multiple_of(r * BLK, BLK), BLK), pl.ds(pl.multiple_of(q * BLK, BLK), BLK)] = total.astype(BF16)
        return c

    lax.fori_loop(0, (targets // BLK) * col_blocks, place, 0)
    degree = jnp.sum(adj[...].astype(F32), axis=1, keepdims=True)
    scale = 1.0 / jnp.maximum(degree, 1.0)
    get_cot.wait()
    w_copy.wait_recv()

    pltpu.make_async_copy(rows_buf.at[pl.ds(0, NDP - 1)], rows_buf.at[pl.ds(0, NDP - 1)], rows_rs).wait()
    sampled = rows_buf[...].reshape(NDP * TILE, fcols)
    self_rows = sampled[:targets]
    neigh = dot(adj[...], sampled) * scale
    x_b[0, :, :fcols] = self_rows
    x_b[1, :, :fcols] = neigh.astype(BF16)
    x_copy = pltpu.make_async_remote_copy(
        x_b, x_p, q_ss.at[1], q_rs.at[1], device_id=(me, mate), device_id_type=MESH
    )
    x_copy.start()

    both = jnp.concatenate([x_b[0], x_b[1]], axis=1)
    for k in CHIPS + (0,):
        chip = (x + k) % NX
        q_own[chip] = dot(both, w_b[core, chip])
    x_copy.wait_recv()
    other = jnp.concatenate([x_p[0], x_p[1]], axis=1)
    for k in CHIPS:
        chip = (x + k) % NX
        p_send[chip] = (q_own[chip] + dot(other, w_p[chip])).astype(BF16)
        pltpu.make_async_remote_copy(
            p_send.at[chip], p_recv.at[x], send_sem.at[3 * CHUNKS], p_rs.at[x],
            device_id=(me, chip * 2 + core), device_id_type=MESH,
        ).start()
    preact = q_own[x] + dot(other, w_p[x]) + bias_v[...]

    xs_t = self_rows.astype(F32).T
    xn_t = neigh.T
    ones = jnp.where(lax.broadcasted_iota(jnp.int32, (TILE, targets), 0) == 0, 1.0, 0.0)
    xt_b[:fcols] = xs_t.astype(BF16)
    xt_b[fcols:fcols + TILE] = ones.astype(BF16)
    xt_b[fcols + TILE:] = xn_t.astype(BF16)

    for k in (1, 3, 2):
        frm = (x + k) % NX
        pltpu.make_async_copy(p_recv.at[frm], p_recv.at[frm], p_rs.at[frm]).wait()
        preact = preact + p_recv[frm].astype(F32)
    alive = jnp.where(lax.broadcasted_iota(jnp.int32, (targets, LANES), 0) < seed_s[0], 1.0, 0.0)
    sigma = jax.nn.sigmoid(preact)
    slope = cot_v[...].astype(F32) * alive * sigma * (1.0 + preact * (1.0 - sigma))
    sl_all[feat] = slope.astype(BF16)

    def slope_copy(which, sem, to):
        return pltpu.make_async_remote_copy(
            sl_all.at[which], sl_all.at[which], sem, sl_rs.at[which],
            device_id=(me, to), device_id_type=MESH,
        )

    for k in CHIPS:
        slope_copy(feat, send_sem.at[3 * CHUNKS + 1], (x + k) % NX * 2 + core).start()
    slope_copy(feat, q_ss.at[2], mate).start()
    hid_v[...] = (preact * sigma * alive).astype(BF16)
    put_hidden = pltpu.make_async_copy(hid_v, hidden_hbm, out_sem.at[0])
    put_hidden.start()

    def line(across, k):
        if across:
            return dp_of((y + k) % NY, z)
        return dp_of(y, (z + k) % NZ)

    class Chunk:
        def __init__(self, n):
            self.low, self.high, self.across = CHUNK_ROWS[n]
            self.send, self.recv, self.own, self.second, self.total = pieces[5 * n:5 * n + 5]
            self.here, self.there = (y, z) if self.across else (z, y)
            self.n = n
            base = 0 if self.low < s_rows else s_rows
            self.out = (n_hbm if self.across else s_hbm).at[:, pl.ds(self.low - base, self.high - self.low)]

        def first(self, at, grad):
            part = grad[self.low:self.high]

            @pl.when(at == self.here)
            def _():
                self.own[...] = part

            @pl.when(at != self.here)
            def _():
                self.send[at] = part.astype(BF16)
                to = dp_of(at, z) if self.across else dp_of(y, at)
                pltpu.make_async_remote_copy(
                    self.send.at[at], self.recv.at[self.here], send_sem.at[self.n], first_rs.at[self.n, self.here],
                    device_id=(to, feat), device_id_type=MESH,
                ).start()

        def add_first(self):
            total = self.own[...]
            for k in RING:
                frm = (self.here - k + NZ) % NZ
                pltpu.make_async_copy(self.recv.at[frm], self.recv.at[frm], first_rs.at[self.n, frm]).wait()
                total = total + self.recv[frm].astype(F32)
            self.second[self.there] = total.astype(BF16)
            for k in RING:
                pltpu.make_async_remote_copy(
                    self.second.at[self.there], self.second.at[self.there],
                    send_sem.at[CHUNKS + self.n], second_rs.at[self.n, self.there],
                    device_id=(line(not self.across, k), feat), device_id_type=MESH,
                ).start()

        def add_second(self):
            for k in RING:
                frm = (self.there - k + NZ) % NZ
                pltpu.make_async_copy(self.second.at[frm], self.second.at[frm], second_rs.at[self.n, frm]).wait()
            total = self.second[0].astype(F32)
            for n in range(1, NZ):
                total = total + self.second[n].astype(F32)
            self.total[...] = total.astype(BF16)
            for k in RING:
                pltpu.make_async_remote_copy(
                    self.total, self.out.at[self.here], send_sem.at[2 * CHUNKS + self.n], third_rs.at[self.n, self.here],
                    device_id=(line(self.across, k), feat), device_id_type=MESH,
                ).start()
            self.keep().start()

        def keep(self):
            return pltpu.make_async_copy(self.total, self.out.at[self.here], out_sem.at[1 + self.n])

        def finish(self):
            for k in RING:
                frm = (self.here - k + NZ) % NZ
                pltpu.make_async_copy(self.out.at[frm], self.out.at[frm], third_rs.at[self.n, frm]).wait()
            self.keep().wait()

    s_rows = fcols + TILE
    chunks = [Chunk(n) for n in range(CHUNKS)]

    def first(block):
        grad = dot(xt_b[...], sl_all[block])
        for chunk in chunks:
            chunk.first(block // 2 + block % 2 * NX, grad)

    def wait_slope(which):
        pltpu.make_async_copy(sl_all.at[which], sl_all.at[which], sl_rs.at[which]).wait()

    first(feat)
    wait_slope(mate)
    first(mate)
    for n, k in enumerate((1, 3, 2)):
        direct = (x + k) % NX * 2 + core
        passed = (x + k) % NX * 2 + 1 - core
        wait_slope(direct)
        slope_copy(direct, q_ss.at[3 + n], mate).start()
        first(direct)
        wait_slope(passed)
        first(passed)

    for chunk in chunks:
        chunk.add_first()
    for chunk in chunks:
        chunk.add_second()
    for chunk in chunks:
        chunk.finish()
    put_hidden.wait()

    def sent(buf, count, sem):
        pltpu.make_async_copy(buf.at[pl.ds(0, count)], buf.at[pl.ds(0, count)], sem).wait()

    sent(ids_y, NY - 1, ids_ss.at[0])
    sent(ids_buf, NZ - 1, ids_ss.at[1])
    sent(rows_send, NDP - 1, rows_ss)
    sent(p_send, NX - 1, send_sem.at[3 * CHUNKS])
    sent(sl_all, NX - 1, send_sem.at[3 * CHUNKS + 1])
    for chunk in chunks:
        sent(chunk.send, NZ - 1, send_sem.at[chunk.n])
        sent(chunk.second, NZ - 1, send_sem.at[CHUNKS + chunk.n])
        sent(chunk.send, NZ - 1, send_sem.at[2 * CHUNKS + chunk.n])
    w_copy.wait_send()
    x_copy.wait_send()
    for c in range(NX):
        sent(sl_all, 1, q_ss.at[2 + c])


def finish(hidden_in, s_in, n_in, hidden_ref, gself_ref, gneigh_ref, gbias_ref, gs_v, gn_v, gb_v, sem):
    fcols = gs_v.shape[0]
    copies = [pltpu.make_async_copy(hidden_in, hidden_ref, sem.at[0])]
    copies[0].start()
    for t in range(NF):
        c = (t % NX) * 2 + t // NX
        gs_v[:, c * LANES:(c + 1) * LANES] = s_in[t][:fcols].astype(F32)
    copies.append(pltpu.make_async_copy(gs_v, gself_ref, sem.at[1]))
    copies[1].start()
    for t in range(NF):
        c = (t % NX) * 2 + t // NX
        gn_v[:, c * LANES:(c + 1) * LANES] = n_in[t].astype(F32)
    copies.append(pltpu.make_async_copy(gn_v, gneigh_ref, sem.at[2]))
    copies[2].start()
    feat = lax.axis_index("feat")
    gb_v[...] = s_in[feat // 2 + feat % 2 * NX][fcols:fcols + TILE].astype(F32)[:1]
    copies.append(pltpu.make_async_copy(gb_v, gbias_ref, sem.at[3]))
    copies[3].start()
    for copy in copies:
        copy.wait()


def on_device(table, node_ids, tiles, tile_rows, tile_cols, tile_count, seed_count, w_self, w_neigh, bias, cotangent):
    fcols = table.shape[1]
    hidden_all = w_self.shape[1]
    targets, hid = cotangent.shape
    s_rows, n_rows = fcols + TILE, fcols
    vmem = pltpu.VMEM
    dma = pltpu.SemaphoreType.DMA
    hbm = pl.BlockSpec(memory_space=pl.ANY)
    scratch = [
        vmem(table.shape[::-1], F32),
        vmem(table.shape[::-1], BF16),
        vmem(tiles.shape, jnp.int32),
        vmem(tiles.shape, F32),
        vmem(w_self.shape, F32),
        vmem(w_neigh.shape, F32),
        vmem((2, NX, 2 * LANES, LANES), BF16),
        vmem((NX, 2 * LANES, LANES), BF16),
        vmem(cotangent.shape, BF16),
        vmem((1, hid), F32),
        pltpu.SMEM(tile_rows.shape, jnp.int32),
        pltpu.SMEM(tile_cols.shape, jnp.int32),
        pltpu.SMEM(tile_count.shape, jnp.int32),
        pltpu.SMEM(seed_count.shape, jnp.int32),
        vmem((NY, 1, LANES), jnp.int32),
        vmem((NZ, NY, 1, LANES), jnp.int32),
        vmem((NDP, TILE, fcols), BF16),
        vmem((NDP, TILE, fcols), BF16),
        vmem((targets, NDP * TILE), BF16),
        vmem((2, targets, LANES), BF16),
        vmem((2, targets, LANES), BF16),
        vmem((s_rows + n_rows, targets), BF16),
        vmem((NX, targets, hid), F32),
        vmem((NX, targets, hid), BF16),
        vmem((NX, targets, hid), BF16),
        vmem((NF, targets, hid), BF16),
        vmem((targets, hid), BF16),
    ]
    for low, high, _ in CHUNK_ROWS:
        rows = high - low
        scratch += [
            vmem((NZ, rows, LANES), BF16),
            vmem((NZ, rows, LANES), BF16),
            vmem((rows, LANES), F32),
            vmem((NZ, rows, LANES), BF16),
            vmem((rows, LANES), BF16),
        ]
    scratch += [
        dma((11,)),
        dma((2,)), dma, dma, dma, dma,
        dma((2 + NX,)), dma((2,)),
        dma((3 * CHUNKS + 2,)),
        dma((NX,)), dma((NF,)),
        dma((CHUNKS, NZ)), dma((CHUNKS, NZ)), dma((CHUNKS, NZ)),
        dma((1 + CHUNKS,)),
    ]
    hidden, s4, n4 = pl.pallas_call(
        kernel,
        out_shape=(
            jax.ShapeDtypeStruct((targets, hid), BF16),
            jax.ShapeDtypeStruct((NZ, s_rows, LANES), BF16),
            jax.ShapeDtypeStruct((NY, n_rows, LANES), BF16),
        ),
        in_specs=[hbm] * 11,
        out_specs=(hbm,) * 3,
        scratch_shapes=scratch,
        compiler_params=pltpu.CompilerParams(
            collective_id=0, has_side_effects=True, vmem_limit_bytes=VMEM_LIMIT
        ),
        cost_estimate=pl.CostEstimate(flops=300_000_000, bytes_accessed=4_000_000, transcendentals=65536),
    )(
        table.T, node_ids.reshape(NY, 1, NZ * TILE), tiles, tile_rows, tile_cols,
        tile_count, seed_count, w_self, w_neigh, bias.reshape(1, hid), cotangent,
    )
    hidden, grad_self, grad_neigh, grad_bias = pl.pallas_call(
        finish,
        out_shape=(
            jax.ShapeDtypeStruct((targets, hid), BF16),
            jax.ShapeDtypeStruct(w_self.shape, F32),
            jax.ShapeDtypeStruct(w_neigh.shape, F32),
            jax.ShapeDtypeStruct((1, hid), F32),
        ),
        in_specs=[pl.BlockSpec(memory_space=pltpu.VMEM)] * 3,
        out_specs=(hbm,) * 4,
        scratch_shapes=[
            vmem(w_self.shape, F32), vmem(w_neigh.shape, F32), vmem((1, hid), F32), dma((4,)),
        ],
    )(hidden, s4, n4)
    return hidden, grad_self, grad_neigh, grad_bias.reshape(hid)


def solution(mesh):
    placed = (
        P("dp", "feat"),
        P("dp"),
        P("dp", None, None),
        P("dp"),
        P("dp"),
        P("dp"),
        P("dp"),
        P("feat", None),
        P("feat", None),
        P("feat"),
        P("dp", "feat"),
    )
    return jax.shard_map(
        on_device,
        mesh=mesh,
        in_specs=placed,
        out_specs=(P("dp", "feat"), P("feat", None), P("feat", None), P("feat")),
        check_vma=False,
    )
```

time: 73.7 us -> 70 us (0.950)
  Pallas kernels: 71.6 us -> 67.1 us
    pallas_call x1, Pallas kernels: 69.5 us -> 65.1 us  [on_device(): pl.pallas_call(kernel, out_shape=(jax.ShapeDtypeStruct((targets, hid), BF...]
where the time goes in v3:
time: 70 us; the launch traced here: 69.1 us
  Pallas kernels  67.1 us (96%)
  between operations  1.93 us (3%)
    pallas_call x1, Pallas kernels, on_device(): pl.pallas_call(kernel, out_shape=(jax.ShapeDtypeStruct((targets, hid), BF...  65.1 us
    pallas_call x1, Pallas kernels, on_device(): pl.pallas_call(finish, out_shape=(jax.ShapeDtypeStruct((targets, hid), BF...  2.02 us

profile of v3, /device:TPU:6, one launch (start us, length us, event | category | flops | bytes accessed | tf_op | source)
XLA Modules:
  0.0 69.1 jit_solution(10351729410343713876)
XLA Ops:
  1.9 65.1 %shard_map.138 = (bf16[256,128]{1,0:T(8,128)(2,1)}, bf16[8,112,128]{2,1,0:T(8,128)(2,1)}, bf16[8,96,128]{2,1,0:T(8,128)(2,1)}) custom-call(f32[96,512]{1,0:T(8,128)} %bitcast.4, s32[8,1,128]{2,1,0:T(1,128)} %bitcast.5, s32[8,128,128]{2,1,0:T(8,128)} %tiles_hbm.1, s32[8]{0:T(128)} %rows_hbm.1, s32[8]{0:T(128)} %cols_hbm.1, s32[1]{0:T(128)S(6)} %copy.15.count_hbm, ...), custom_call_target="tpu_custom_call" | custom-call | flops 300000000 | bytes 4000000 | tf_op jit(solution)/shard_map/pallas_call | solution.py:427
  67.1 2.0 %shard_map.139 = (bf16[256,128]{1,0:T(8,128)(2,1)}, f32[96,1024]{1,0:T(8,128)}, f32[96,1024]{1,0:T(8,128)}, f32[1,128]{1,0:T(1,128)}) custom-call(bf16[256,128]{1,0:T(8,128)(2,1)} %get-tuple-element.11.hidden_in, bf16[8,112,128]{2,1,0:T(8,128)(2,1)} %get-tuple-element.12.s_in, bf16[8,96,128]{2,1,0:T(8,128)(2,1)} %get-tuple-element.13.n_in), custom_call_target="tpu_custom_call" | custom-call | tf_op jit(solution)/shard_map/pallas_call | solution.py:445

commit v4 on v3

--- a/solution.py
+++ b/solution.py
@@ -17,9 +17,17 @@
 
 
 RING = (4, 5, 3, 6, 2, 7, 1)
+
+
+def hops(offset):
+    return min(offset[0], NY - offset[0]) + min(offset[1], NZ - offset[1])
+
+
+FARTHEST = sorted(((a, b) for a in range(NY) for b in range(NZ) if a or b), key=lambda o: (-hops(o), o))
 CHIPS = (2, 1, 3)
 CHUNK_ROWS = ((0, 64, False), (112, 160, True), (64, 112, False), (160, 208, True))
 CHUNKS = len(CHUNK_ROWS)
+HALVES = 2
 
 
 def dot(a, b):
@@ -34,13 +42,13 @@
     table_hbm, ids_hbm, tiles_hbm, rows_hbm, cols_hbm, count_hbm, seed_hbm, ws_hbm, wn_hbm, bias_hbm, cot_hbm,
     hidden_hbm, s_hbm, n_hbm,
     table_f, table_b, tiles_i, tiles_f, ws_f, wn_f, w_b, w_p, cot_v, bias_v, rows_s, cols_s, count_s, seed_s,
-    ids_y, ids_buf, rows_send, rows_buf, adj, x_b, x_p, xt_b,
+    ids_v, ids_y, ids_buf, rows_send, rows_buf, adj, x_b, x_p, xt_b,
     q_own, p_send, p_recv, sl_all, hid_v,
     *rest,
 ):
     pieces, rest = rest[:5 * CHUNKS], rest[5 * CHUNKS:]
     (
-        loc_sem, ids_ss, idy_rs, idz_rs, rows_ss, rows_rs, q_ss, q_rs, send_sem, p_rs, sl_rs, first_rs, second_rs, third_rs,
+        loc_sem, ids_ss, idy_rs, idz_rs, rows_ss, rows_rs, q_ss, q_rs, f_ss, send_sem, p_rs, sl_rs, first_rs, second_rs, third_rs,
         out_sem,
     ) = rest
     me = lax.axis_index("dp")
@@ -56,7 +64,7 @@
     def dp_of(yy, zz):
         return yy * NZ + zz
 
-    own_ids = pltpu.make_async_copy(ids_hbm.at[y], ids_y.at[y], loc_sem.at[0])
+    own_ids = pltpu.make_async_copy(ids_hbm, ids_v, loc_sem.at[0])
     get_table = pltpu.make_async_copy(table_hbm, table_f, loc_sem.at[1])
     get_ws = pltpu.make_async_copy(ws_hbm, ws_f, loc_sem.at[2])
     get_wn = pltpu.make_async_copy(wn_hbm, wn_f, loc_sem.at[3])
@@ -81,10 +89,11 @@
     pl.semaphore_signal(barrier, inc=1, device_id=(me, mate), device_id_type=MESH)
     pl.semaphore_wait(barrier, NZ - 1 + NY - 1 + NX)
 
+    own_ids.wait()
     for k in RING:
         yy = (y + k) % NY
         pltpu.make_async_remote_copy(
-            ids_hbm.at[yy], ids_y.at[y], ids_ss.at[0], idy_rs,
+            ids_v.at[yy], ids_y.at[y], ids_ss.at[0], idy_rs,
             device_id=(dp_of(yy, z), feat), device_id_type=MESH,
         ).start()
     get_table.start()
@@ -94,7 +103,7 @@
     for copy in small:
         copy.start()
     get_cot.start()
-    own_ids.wait()
+    ids_y[y] = ids_v[y]
     pltpu.make_async_copy(ids_y.at[pl.ds(0, NY - 1)], ids_y.at[pl.ds(0, NY - 1)], idy_rs).wait()
     for k in RING:
         pltpu.make_async_remote_copy(
@@ -122,21 +131,21 @@
             hot = jnp.where(column == row_of, 1.0, 0.0).astype(BF16)
             found = dot_t(hot, table_b[...]).astype(BF16)
             rows_send[pl.ds(yy * NZ, NZ)] = found.reshape(NZ, TILE, fcols)
-        for dz in RING + (0,):
-            zz = (z + dz) % NZ
-            for yy in pair:
-                to = dp_of(yy, zz)
-                copy = pltpu.make_async_remote_copy(
-                    rows_send.at[to], rows_buf.at[me], rows_ss, rows_rs,
-                    device_id=(to, feat), device_id_type=MESH,
-                )
-                if dz == 0:
-                    pl.when(to != me)(copy.start)
-                else:
-                    copy.start()
         return c
 
-    lax.fori_loop(0, NY // 2, gather, 0)
+    def send_rows(chosen):
+        for dy, dz in chosen:
+            to = dp_of((y + dy) % NY, (z + dz) % NZ)
+            pltpu.make_async_remote_copy(
+                rows_send.at[to], rows_buf.at[me], rows_ss, rows_rs,
+                device_id=(to, feat), device_id_type=MESH,
+            ).start()
+
+    lax.fori_loop(0, 2, gather, 0)
+    early = [o for o in FARTHEST if o[0] in (3, 4, 5, 6) and hops(o) > 5]
+    send_rows(early)
+    lax.fori_loop(2, NY // 2, gather, 0)
+    send_rows([o for o in FARTHEST if o not in early])
     rows_buf[me] = rows_send[me]
 
     get_ws.wait()
@@ -192,13 +201,17 @@
         q_own[chip] = dot(both, w_b[core, chip])
     x_copy.wait_recv()
     other = jnp.concatenate([x_p[0], x_p[1]], axis=1)
-    for k in CHIPS:
-        chip = (x + k) % NX
-        p_send[chip] = (q_own[chip] + dot(other, w_p[chip])).astype(BF16)
-        pltpu.make_async_remote_copy(
-            p_send.at[chip], p_recv.at[x], send_sem.at[3 * CHUNKS], p_rs.at[x],
-            device_id=(me, chip * 2 + core), device_id_type=MESH,
-        ).start()
+    half = targets // HALVES
+    for h in range(HALVES):
+        low = h * half
+        for k in CHIPS:
+            chip = (x + k) % NX
+            own = q_own[chip, low:low + half]
+            p_send[h, chip] = (own + dot(other[low:low + half], w_p[chip])).astype(BF16)
+            pltpu.make_async_remote_copy(
+                p_send.at[h, chip], p_recv.at[h, x], send_sem.at[3 * CHUNKS + h], p_rs.at[h, x],
+                device_id=(me, chip * 2 + core), device_id_type=MESH,
+            ).start()
     preact = q_own[x] + dot(other, w_p[x]) + bias_v[...]
 
     xs_t = self_rows.astype(F32).T
@@ -208,25 +221,31 @@
     xt_b[fcols:fcols + TILE] = ones.astype(BF16)
     xt_b[fcols + TILE:] = xn_t.astype(BF16)
 
-    for k in (1, 3, 2):
-        frm = (x + k) % NX
-        pltpu.make_async_copy(p_recv.at[frm], p_recv.at[frm], p_rs.at[frm]).wait()
-        preact = preact + p_recv[frm].astype(F32)
-    alive = jnp.where(lax.broadcasted_iota(jnp.int32, (targets, LANES), 0) < seed_s[0], 1.0, 0.0)
-    sigma = jax.nn.sigmoid(preact)
-    slope = cot_v[...].astype(F32) * alive * sigma * (1.0 + preact * (1.0 - sigma))
-    sl_all[feat] = slope.astype(BF16)
-
-    def slope_copy(which, sem, to):
+    def slope_copy(which, h, sem, to):
         return pltpu.make_async_remote_copy(
-            sl_all.at[which], sl_all.at[which], sem, sl_rs.at[which],
+            sl_all.at[which, h], sl_all.at[which, h], sem, sl_rs.at[which, h],
             device_id=(me, to), device_id_type=MESH,
         )
 
-    for k in CHIPS:
-        slope_copy(feat, send_sem.at[3 * CHUNKS + 1], (x + k) % NX * 2 + core).start()
-    slope_copy(feat, q_ss.at[2], mate).start()
-    hid_v[...] = (preact * sigma * alive).astype(BF16)
+    def activate(h):
+        low = h * half
+        total = preact[low:low + half]
+        for k in (1, 3, 2):
+            frm = (x + k) % NX
+            pltpu.make_async_copy(p_recv.at[h, frm], p_recv.at[h, frm], p_rs.at[h, frm]).wait()
+            total = total + p_recv[h, frm].astype(F32)
+        row = low + lax.broadcasted_iota(jnp.int32, (half, LANES), 0)
+        alive = jnp.where(row < seed_s[0], 1.0, 0.0)
+        sigma = jax.nn.sigmoid(total)
+        slope = cot_v[low:low + half].astype(F32) * alive * sigma * (1.0 + total * (1.0 - sigma))
+        sl_all[feat, h] = slope.astype(BF16)
+        for k in CHIPS:
+            slope_copy(feat, h, send_sem.at[3 * CHUNKS + HALVES + h], (x + k) % NX * 2 + core).start()
+        slope_copy(feat, h, f_ss.at[0, h], mate).start()
+        hid_v[low:low + half] = (total * sigma * alive).astype(BF16)
+
+    for h in range(HALVES):
+        activate(h)
     put_hidden = pltpu.make_async_copy(hid_v, hidden_hbm, out_sem.at[0])
     put_hidden.start()
 
@@ -302,23 +321,26 @@
     chunks = [Chunk(n) for n in range(CHUNKS)]
 
     def first(block):
-        grad = dot(xt_b[...], sl_all[block])
+        grad = dot(xt_b[...], sl_all[block].reshape(targets, LANES))
         for chunk in chunks:
             chunk.first(block // 2 + block % 2 * NX, grad)
 
-    def wait_slope(which):
-        pltpu.make_async_copy(sl_all.at[which], sl_all.at[which], sl_rs.at[which]).wait()
+    def wait_slope(which, h):
+        pltpu.make_async_copy(sl_all.at[which, h], sl_all.at[which, h], sl_rs.at[which, h]).wait()
 
     first(feat)
-    wait_slope(mate)
+    for h in range(HALVES):
+        wait_slope(mate, h)
     first(mate)
     for n, k in enumerate((1, 3, 2)):
         direct = (x + k) % NX * 2 + core
         passed = (x + k) % NX * 2 + 1 - core
-        wait_slope(direct)
-        slope_copy(direct, q_ss.at[3 + n], mate).start()
+        for h in range(HALVES):
+            wait_slope(direct, h)
+            slope_copy(direct, h, f_ss.at[1 + n, h], mate).start()
         first(direct)
-        wait_slope(passed)
+        for h in range(HALVES):
+            wait_slope(passed, h)
         first(passed)
 
     for chunk in chunks:
@@ -335,8 +357,9 @@
     sent(ids_y, NY - 1, ids_ss.at[0])
     sent(ids_buf, NZ - 1, ids_ss.at[1])
     sent(rows_send, NDP - 1, rows_ss)
-    sent(p_send, NX - 1, send_sem.at[3 * CHUNKS])
-    sent(sl_all, NX - 1, send_sem.at[3 * CHUNKS + 1])
+    for h in range(HALVES):
+        sent(p_send.at[h], NX - 1, send_sem.at[3 * CHUNKS + h])
+        sent(p_send.at[h], NX - 1, send_sem.at[3 * CHUNKS + HALVES + h])
     for chunk in chunks:
         sent(chunk.send, NZ - 1, send_sem.at[chunk.n])
         sent(chunk.second, NZ - 1, send_sem.at[CHUNKS + chunk.n])
@@ -344,28 +367,44 @@
     w_copy.wait_send()
     x_copy.wait_send()
     for c in range(NX):
-        sent(sl_all, 1, q_ss.at[2 + c])
-
-
-def finish(hidden_in, s_in, n_in, hidden_ref, gself_ref, gneigh_ref, gbias_ref, gs_v, gn_v, gb_v, sem):
+        for h in range(HALVES):
+            pltpu.make_async_copy(sl_all.at[c, h], sl_all.at[c, h], f_ss.at[c, h]).wait()
+
+
+def finish(
+    hidden_in, s_in, n_in, hidden_ref, gself_ref, gneigh_ref, gbias_ref, h_v, s_v, n_v, gs_v, gn_v, gb_v, in_sem, out_sem
+):
     fcols = gs_v.shape[0]
-    copies = [pltpu.make_async_copy(hidden_in, hidden_ref, sem.at[0])]
-    copies[0].start()
-    for t in range(NF):
-        c = (t % NX) * 2 + t // NX
-        gs_v[:, c * LANES:(c + 1) * LANES] = s_in[t][:fcols].astype(F32)
-    copies.append(pltpu.make_async_copy(gs_v, gself_ref, sem.at[1]))
-    copies[1].start()
-    for t in range(NF):
-        c = (t % NX) * 2 + t // NX
-        gn_v[:, c * LANES:(c + 1) * LANES] = n_in[t].astype(F32)
-    copies.append(pltpu.make_async_copy(gn_v, gneigh_ref, sem.at[2]))
-    copies[2].start()
+    gets = []
+    for n, (src, dst) in enumerate(((s_in, s_v), (n_in, n_v))):
+        for part in range(2):
+            rows = pl.ds(part * NX, NX)
+            gets.append(pltpu.make_async_copy(src.at[rows], dst.at[rows], in_sem.at[n * 2 + part]))
+    for copy in gets:
+        copy.start()
+    get_hidden = pltpu.make_async_copy(hidden_in, h_v, in_sem.at[4])
+    get_hidden.start()
+    puts = []
+
+    def put(src, dst):
+        puts.append(pltpu.make_async_copy(src, dst, out_sem.at[len(puts)]))
+        puts[-1].start()
+
     feat = lax.axis_index("feat")
-    gb_v[...] = s_in[feat // 2 + feat % 2 * NX][fcols:fcols + TILE].astype(F32)[:1]
-    copies.append(pltpu.make_async_copy(gb_v, gbias_ref, sem.at[3]))
-    copies[3].start()
-    for copy in copies:
+    for src, dst, base, out in ((s_v, gs_v, 0, gself_ref), (n_v, gn_v, 2, gneigh_ref)):
+        for part in range(2):
+            gets[base + part].wait()
+            for t in range(part * NX, part * NX + NX):
+                c = (t % NX) * 2 + t // NX
+                dst[:, c * LANES:(c + 1) * LANES] = src[t][:fcols].astype(F32)
+        if base == 0:
+            gb_v[...] = s_v[feat // 2 + feat % 2 * NX][fcols:fcols + TILE].astype(F32)[:1]
+            put(gb_v, gbias_ref)
+        put(dst, out)
+        if base == 0:
+            get_hidden.wait()
+            put(h_v, hidden_ref)
+    for copy in puts:
         copy.wait()
 
 
@@ -393,6 +432,7 @@
         pltpu.SMEM(tile_count.shape, jnp.int32),
         pltpu.SMEM(seed_count.shape, jnp.int32),
         vmem((NY, 1, LANES), jnp.int32),
+        vmem((NY, 1, LANES), jnp.int32),
         vmem((NZ, NY, 1, LANES), jnp.int32),
         vmem((NDP, TILE, fcols), BF16),
         vmem((NDP, TILE, fcols), BF16),
@@ -401,9 +441,9 @@
         vmem((2, targets, LANES), BF16),
         vmem((s_rows + n_rows, targets), BF16),
         vmem((NX, targets, hid), F32),
-        vmem((NX, targets, hid), BF16),
-        vmem((NX, targets, hid), BF16),
-        vmem((NF, targets, hid), BF16),
+        vmem((HALVES, NX, targets // HALVES, hid), BF16),
+        vmem((HALVES, NX, targets // HALVES, hid), BF16),
+        vmem((NF, HALVES, targets // HALVES, hid), BF16),
         vmem((targets, hid), BF16),
     ]
     for low, high, _ in CHUNK_ROWS:
@@ -418,9 +458,9 @@
     scratch += [
         dma((11,)),
         dma((2,)), dma, dma, dma, dma,
-        dma((2 + NX,)), dma((2,)),
-        dma((3 * CHUNKS + 2,)),
-        dma((NX,)), dma((NF,)),
+        dma((2,)), dma((2,)), dma((NX, HALVES)),
+        dma((3 * CHUNKS + 2 * HALVES,)),
+        dma((HALVES, NX)), dma((NF, HALVES)),
         dma((CHUNKS, NZ)), dma((CHUNKS, NZ)), dma((CHUNKS, NZ)),
         dma((1 + CHUNKS,)),
     ]
@@ -450,10 +490,11 @@
             jax.ShapeDtypeStruct(w_neigh.shape, F32),
             jax.ShapeDtypeStruct((1, hid), F32),
         ),
-        in_specs=[pl.BlockSpec(memory_space=pltpu.VMEM)] * 3,
+        in_specs=[hbm] * 3,
         out_specs=(hbm,) * 4,
         scratch_shapes=[
-            vmem(w_self.shape, F32), vmem(w_neigh.shape, F32), vmem((1, hid), F32), dma((4,)),
+            vmem((targets, hid), BF16), vmem((NZ, s_rows, LANES), BF16), vmem((NY, n_rows, LANES), BF16),
+            vmem(w_self.shape, F32), vmem(w_neigh.shape, F32), vmem((1, hid), F32), dma((5,)), dma((4,)),
         ],
     )(hidden, s4, n4)
     return hidden, grad_self, grad_neigh, grad_bias.reshape(hid)

time: 70 us -> 68.6 us (0.980); the launches traced: 69.1 us -> 68.5 us
  no operation moved by 1% of the time
where the time goes in v4:
time: 68.6 us; the launch traced here: 68.5 us
  Pallas kernels  66.5 us (97%)
  between operations  1.93 us (3%)
    pallas_call x1, Pallas kernels, on_device(): pl.pallas_call(kernel, out_shape=(jax.ShapeDtypeStruct((targets, hid), BF...  64.6 us
    pallas_call x1, Pallas kernels, on_device(): pl.pallas_call(finish, out_shape=(jax.ShapeDtypeStruct((targets, hid), BF...  1.95 us

profile of v4, /device:TPU:6, one launch (start us, length us, event | category | flops | bytes accessed | tf_op | source)
XLA Modules:
  0.0 68.5 jit_solution(443252356026141500)
XLA Ops:
  1.9 64.6 %shard_map.138 = (bf16[256,128]{1,0:T(8,128)(2,1)}, bf16[8,112,128]{2,1,0:T(8,128)(2,1)}, bf16[8,96,128]{2,1,0:T(8,128)(2,1)}) custom-call(f32[96,512]{1,0:T(8,128)} %bitcast.4, s32[8,1,128]{2,1,0:T(1,128)} %bitcast.5, s32[8,128,128]{2,1,0:T(8,128)} %tiles_hbm.1, s32[8]{0:T(128)} %rows_hbm.1, s32[8]{0:T(128)} %cols_hbm.1, s32[1]{0:T(128)S(6)} %copy.15.count_hbm, ...), custom_call_target="tpu_custom_call" | custom-call | flops 300000000 | bytes 4000000 | tf_op jit(solution)/shard_map/pallas_call | solution.py:467
  66.5 2.0 %shard_map.139 = (bf16[256,128]{1,0:T(8,128)(2,1)}, f32[96,1024]{1,0:T(8,128)}, f32[96,1024]{1,0:T(8,128)}, f32[1,128]{1,0:T(1,128)}) custom-call(bf16[256,128]{1,0:T(8,128)(2,1)} %get-tuple-element.11.hidden_in, bf16[8,112,128]{2,1,0:T(8,128)(2,1)} %get-tuple-element.12.s_in, bf16[8,96,128]{2,1,0:T(8,128)(2,1)} %get-tuple-element.13.n_in), custom_call_target="tpu_custom_call" | custom-call | tf_op jit(solution)/shard_map/pallas_call | solution.py:485

commit v5 on v4

--- a/solution.py
+++ b/solution.py
@@ -97,12 +97,6 @@
             device_id=(dp_of(yy, z), feat), device_id_type=MESH,
         ).start()
     get_table.start()
-    get_ws.start()
-    get_wn.start()
-    get_tiles.start()
-    for copy in small:
-        copy.start()
-    get_cot.start()
     ids_y[y] = ids_v[y]
     pltpu.make_async_copy(ids_y.at[pl.ds(0, NY - 1)], ids_y.at[pl.ds(0, NY - 1)], idy_rs).wait()
     for k in RING:
@@ -146,6 +140,12 @@
     send_rows(early)
     lax.fori_loop(2, NY // 2, gather, 0)
     send_rows([o for o in FARTHEST if o not in early])
+    get_ws.start()
+    get_wn.start()
+    get_tiles.start()
+    for copy in small:
+        copy.start()
+    get_cot.start()
     rows_buf[me] = rows_send[me]
 
     get_ws.wait()
@@ -187,19 +187,24 @@
     pltpu.make_async_copy(rows_buf.at[pl.ds(0, NDP - 1)], rows_buf.at[pl.ds(0, NDP - 1)], rows_rs).wait()
     sampled = rows_buf[...].reshape(NDP * TILE, fcols)
     self_rows = sampled[:targets]
+    x_b[0, :, :fcols] = self_rows
+    x_copies = [
+        pltpu.make_async_remote_copy(
+            x_b.at[n], x_p.at[n], q_ss.at[1 + n], q_rs.at[1 + n], device_id=(me, mate), device_id_type=MESH
+        )
+        for n in range(2)
+    ]
+    x_copies[0].start()
     neigh = dot(adj[...], sampled) * scale
-    x_b[0, :, :fcols] = self_rows
     x_b[1, :, :fcols] = neigh.astype(BF16)
-    x_copy = pltpu.make_async_remote_copy(
-        x_b, x_p, q_ss.at[1], q_rs.at[1], device_id=(me, mate), device_id_type=MESH
-    )
-    x_copy.start()
+    x_copies[1].start()
 
     both = jnp.concatenate([x_b[0], x_b[1]], axis=1)
     for k in CHIPS + (0,):
         chip = (x + k) % NX
         q_own[chip] = dot(both, w_b[core, chip])
-    x_copy.wait_recv()
+    for copy in x_copies:
+        copy.wait_recv()
     other = jnp.concatenate([x_p[0], x_p[1]], axis=1)
     half = targets // HALVES
     for h in range(HALVES):
@@ -365,7 +370,8 @@
         sent(chunk.second, NZ - 1, send_sem.at[CHUNKS + chunk.n])
         sent(chunk.send, NZ - 1, send_sem.at[2 * CHUNKS + chunk.n])
     w_copy.wait_send()
-    x_copy.wait_send()
+    for copy in x_copies:
+        copy.wait_send()
     for c in range(NX):
         for h in range(HALVES):
             pltpu.make_async_copy(sl_all.at[c, h], sl_all.at[c, h], f_ss.at[c, h]).wait()
@@ -458,7 +464,7 @@
     scratch += [
         dma((11,)),
         dma((2,)), dma, dma, dma, dma,
-        dma((2,)), dma((2,)), dma((NX, HALVES)),
+        dma((3,)), dma((3,)), dma((NX, HALVES)),
         dma((3 * CHUNKS + 2 * HALVES,)),
         dma((HALVES, NX)), dma((NF, HALVES)),
         dma((CHUNKS, NZ)), dma((CHUNKS, NZ)), dma((CHUNKS, NZ)),

time: 68.6 us -> 68.5 us (level)
  no operation moved by 1% of the time
where the time goes in v5:
time: 68.5 us; the launch traced here: 68.3 us
  Pallas kernels  66.4 us (97%)
  between operations  1.93 us (3%)
    pallas_call x1, Pallas kernels, on_device(): pl.pallas_call(kernel, out_shape=(jax.ShapeDtypeStruct((targets, hid), BF...  64.4 us
    pallas_call x1, Pallas kernels, on_device(): pl.pallas_call(finish, out_shape=(jax.ShapeDtypeStruct((targets, hid), BF...  1.95 us

profile of v5, /device:TPU:6, one launch (start us, length us, event | category | flops | bytes accessed | tf_op | source)
XLA Modules:
  0.0 68.3 jit_solution(1318695334222681926)
XLA Ops:
  1.9 64.4 %shard_map.138 = (bf16[256,128]{1,0:T(8,128)(2,1)}, bf16[8,112,128]{2,1,0:T(8,128)(2,1)}, bf16[8,96,128]{2,1,0:T(8,128)(2,1)}) custom-call(f32[96,512]{1,0:T(8,128)} %bitcast.4, s32[8,1,128]{2,1,0:T(1,128)} %bitcast.5, s32[8,128,128]{2,1,0:T(8,128)} %tiles_hbm.1, s32[8]{0:T(128)} %rows_hbm.1, s32[8]{0:T(128)} %cols_hbm.1, s32[1]{0:T(128)S(6)} %copy.15.count_hbm, ...), custom_call_target="tpu_custom_call" | custom-call | flops 300000000 | bytes 4000000 | tf_op jit(solution)/shard_map/pallas_call | solution.py:473
  66.3 2.0 %shard_map.139 = (bf16[256,128]{1,0:T(8,128)(2,1)}, f32[96,1024]{1,0:T(8,128)}, f32[96,1024]{1,0:T(8,128)}, f32[1,128]{1,0:T(1,128)}) custom-call(bf16[256,128]{1,0:T(8,128)(2,1)} %get-tuple-element.11.hidden_in, bf16[8,112,128]{2,1,0:T(8,128)(2,1)} %get-tuple-element.12.s_in, bf16[8,96,128]{2,1,0:T(8,128)(2,1)} %get-tuple-element.13.n_in), custom_call_target="tpu_custom_call" | custom-call | tf_op jit(solution)/shard_map/pallas_call | solution.py:491

commit v6 on v4

--- a/solution.py
+++ b/solution.py
@@ -347,8 +347,6 @@
         chunk.add_first()
     for chunk in chunks:
         chunk.add_second()
-    for chunk in chunks:
-        chunk.finish()
     put_hidden.wait()
 
     def sent(buf, count, sem):
@@ -363,12 +361,15 @@
     for chunk in chunks:
         sent(chunk.send, NZ - 1, send_sem.at[chunk.n])
         sent(chunk.second, NZ - 1, send_sem.at[CHUNKS + chunk.n])
-        sent(chunk.send, NZ - 1, send_sem.at[2 * CHUNKS + chunk.n])
     w_copy.wait_send()
     x_copy.wait_send()
     for c in range(NX):
         for h in range(HALVES):
             pltpu.make_async_copy(sl_all.at[c, h], sl_all.at[c, h], f_ss.at[c, h]).wait()
+    for chunk in chunks:
+        chunk.finish()
+    for chunk in chunks:
+        sent(chunk.send, NZ - 1, send_sem.at[2 * CHUNKS + chunk.n])
 
 
 def finish(

time: 68.6 us -> 68.6 us (level)
  no operation moved by 1% of the time
where the time goes in v6:
time: 68.6 us; the launch traced here: 68.4 us
  Pallas kernels  66.5 us (97%)
  between operations  1.93 us (3%)
    pallas_call x1, Pallas kernels, on_device(): pl.pallas_call(kernel, out_shape=(jax.ShapeDtypeStruct((targets, hid), BF...  64.5 us
    pallas_call x1, Pallas kernels, on_device(): pl.pallas_call(finish, out_shape=(jax.ShapeDtypeStruct((targets, hid), BF...  1.95 us

profile of v6, /device:TPU:6, one launch (start us, length us, event | category | flops | bytes accessed | tf_op | source)
XLA Modules:
  0.0 68.4 jit_solution(7229826053648676449)
XLA Ops:
  1.9 64.5 %shard_map.138 = (bf16[256,128]{1,0:T(8,128)(2,1)}, bf16[8,112,128]{2,1,0:T(8,128)(2,1)}, bf16[8,96,128]{2,1,0:T(8,128)(2,1)}) custom-call(f32[96,512]{1,0:T(8,128)} %bitcast.4, s32[8,1,128]{2,1,0:T(1,128)} %bitcast.5, s32[8,128,128]{2,1,0:T(8,128)} %tiles_hbm.1, s32[8]{0:T(128)} %rows_hbm.1, s32[8]{0:T(128)} %cols_hbm.1, s32[1]{0:T(128)S(6)} %copy.15.count_hbm, ...), custom_call_target="tpu_custom_call" | custom-call | flops 300000000 | bytes 4000000 | tf_op jit(solution)/shard_map/pallas_call | solution.py:468
  66.5 2.0 %shard_map.139 = (bf16[256,128]{1,0:T(8,128)(2,1)}, f32[96,1024]{1,0:T(8,128)}, f32[96,1024]{1,0:T(8,128)}, f32[1,128]{1,0:T(1,128)}) custom-call(bf16[256,128]{1,0:T(8,128)(2,1)} %get-tuple-element.11.hidden_in, bf16[8,112,128]{2,1,0:T(8,128)(2,1)} %get-tuple-element.12.s_in, bf16[8,96,128]{2,1,0:T(8,128)(2,1)} %get-tuple-element.13.n_in), custom_call_target="tpu_custom_call" | custom-call | tf_op jit(solution)/shard_map/pallas_call | solution.py:486

commit v7 on v6

--- a/solution.py
+++ b/solution.py
@@ -332,16 +332,19 @@
     for h in range(HALVES):
         wait_slope(mate, h)
     first(mate)
-    for n, k in enumerate((1, 3, 2)):
-        direct = (x + k) % NX * 2 + core
-        passed = (x + k) % NX * 2 + 1 - core
-        for h in range(HALVES):
-            wait_slope(direct, h)
-            slope_copy(direct, h, f_ss.at[1 + n, h], mate).start()
-        first(direct)
-        for h in range(HALVES):
-            wait_slope(passed, h)
-        first(passed)
+    for group in ((1, 3), (2,)):
+        for k in group:
+            direct = (x + k) % NX * 2 + core
+            for h in range(HALVES):
+                wait_slope(direct, h)
+                slope_copy(direct, h, f_ss.at[k, h], mate).start()
+        for k in group:
+            first((x + k) % NX * 2 + core)
+        for k in group:
+            passed = (x + k) % NX * 2 + 1 - core
+            for h in range(HALVES):
+                wait_slope(passed, h)
+            first(passed)
 
     for chunk in chunks:
         chunk.add_first()

time: 68.6 us -> 68.6 us (level)
  no operation moved by 1% of the time
where the time goes in v7:
time: 68.6 us; the launch traced here: 67.9 us
  Pallas kernels  65.9 us (96%)
  between operations  1.93 us (3%)
    pallas_call x1, Pallas kernels, on_device(): pl.pallas_call(kernel, out_shape=(jax.ShapeDtypeStruct((targets, hid), BF...  64 us
    pallas_call x1, Pallas kernels, on_device(): pl.pallas_call(finish, out_shape=(jax.ShapeDtypeStruct((targets, hid), BF...  1.95 us

profile of v7, /device:TPU:6, one launch (start us, length us, event | category | flops | bytes accessed | tf_op | source)
XLA Modules:
  0.0 67.9 jit_solution(16477579632642667829)
XLA Ops:
  1.9 64.0 %shard_map.138 = (bf16[256,128]{1,0:T(8,128)(2,1)}, bf16[8,112,128]{2,1,0:T(8,128)(2,1)}, bf16[8,96,128]{2,1,0:T(8,128)(2,1)}) custom-call(f32[96,512]{1,0:T(8,128)} %bitcast.4, s32[8,1,128]{2,1,0:T(1,128)} %bitcast.5, s32[8,128,128]{2,1,0:T(8,128)} %tiles_hbm.1, s32[8]{0:T(128)} %rows_hbm.1, s32[8]{0:T(128)} %cols_hbm.1, s32[1]{0:T(128)S(6)} %copy.15.count_hbm, ...), custom_call_target="tpu_custom_call" | custom-call | flops 300000000 | bytes 4000000 | tf_op jit(solution)/shard_map/pallas_call | solution.py:471
  65.9 2.0 %shard_map.139 = (bf16[256,128]{1,0:T(8,128)(2,1)}, f32[96,1024]{1,0:T(8,128)}, f32[96,1024]{1,0:T(8,128)}, f32[1,128]{1,0:T(1,128)}) custom-call(bf16[256,128]{1,0:T(8,128)(2,1)} %get-tuple-element.11.hidden_in, bf16[8,112,128]{2,1,0:T(8,128)(2,1)} %get-tuple-element.12.s_in, bf16[8,96,128]{2,1,0:T(8,128)(2,1)} %get-tuple-element.13.n_in), custom_call_target="tpu_custom_call" | custom-call | tf_op jit(solution)/shard_map/pallas_call | solution.py:489
